TPU v7x, 32 devices: a whole 2x2x4 slice. The times are simulated.
32 devices in a mesh: dp: 4 (over y, core), fsdp: 8 (over z, x).
Axes of the slice: x: 2, y: 2, z: 4, core: 2. Of those that a mesh axis runs over, the one named last changes fastest.
Arguments:
- block_input: bfloat16 [32, 1024, 1280], P(('dp', 'fsdp')), may hold values from -6 to 6
- cotangent: bfloat16 [32, 1024, 1280], P(('dp', 'fsdp')), may hold values from -6 to 6
- protein_lengths: int32 [32, 4], P(('dp', 'fsdp')), may hold values from 1 to 512, 1024 in all within a row
- weight_in: float32 [1280, 640], P('fsdp', 'dp'), may hold values from -0.15625 to 0.15625
- moment_in: float32 [1280, 640], P('fsdp', 'dp'), may hold values from -1 to 1
- square_in: float32 [1280, 640], P('fsdp', 'dp'), may hold values from 0 to 1, as said below
- weight_conv: float32 [5, 640, 640], P(None, 'fsdp', 'dp'), may hold values from -0.109375 to 0.109375
- moment_conv: float32 [5, 640, 640], P(None, 'fsdp', 'dp'), may hold values from -1 to 1
- square_conv: float32 [5, 640, 640], P(None, 'fsdp', 'dp'), may hold values from 0 to 1, as said below
- weight_out: float32 [640, 1280], P('fsdp', 'dp'), may hold values from -0.25 to 0.25
- moment_out: float32 [640, 1280], P('fsdp', 'dp'), may hold values from -1 to 1
- square_out: float32 [640, 1280], P('fsdp', 'dp'), may hold values from 0 to 1, as said below
- vectors: float32 [7680], replicated, may hold values from -2 to 4, as said below
- moment_vectors: float32 [7680], replicated, may hold values from -1 to 1
- square_vectors: float32 [7680], replicated, may hold values from 0 to 1, as said below
Outputs:
- block_output: bfloat16 [32, 1024, 1280], P(('dp', 'fsdp'))
- input_grad: bfloat16 [32, 1024, 1280], P(('dp', 'fsdp'))
- grad_norm: float32 [], replicated
- new_weight_in: float32 [1280, 640], P('fsdp', 'dp')
- new_moment_in: float32 [1280, 640], P('fsdp', 'dp')
- new_square_in: float32 [1280, 640], P('fsdp', 'dp')
- new_weight_conv: float32 [5, 640, 640], P(None, 'fsdp', 'dp')
- new_moment_conv: float32 [5, 640, 640], P(None, 'fsdp', 'dp')
- new_square_conv: float32 [5, 640, 640], P(None, 'fsdp', 'dp')
- new_weight_out: float32 [640, 1280], P('fsdp', 'dp')
- new_moment_out: float32 [640, 1280], P('fsdp', 'dp')
- new_square_out: float32 [640, 1280], P('fsdp', 'dp')
- new_vectors: float32 [7680], replicated
- new_moment_vectors: float32 [7680], replicated
- new_square_vectors: float32 [7680], replicated
Inputs may be any that keep to these rules, and one draw needn't show every extreme that they name: `vectors`: gains positive, shifts and biases of both signs. `square_in`: positive. `square_conv`: positive. `square_out`: positive. `square_vectors`: positive.
All inputs are finite; a program needn't handle non-finite values.
Results may differ from a plain program's by a relative error of at most 0.02.
Values may be sent and summed in bfloat16 or wider, within the bound.
No kernel may reach another device: no remote copies, remote signals or barrier semaphores. Data moves between devices by JAX's collectives and lax.ppermute only.
A program may use at most 128 MiB of HBM per device.

v0:
```python
import functools

import jax
import jax.numpy as jnp
from jax import lax
from jax.experimental import pallas as pl
from jax.experimental.pallas import tpu as pltpu
from jax.sharding import PartitionSpec as P

D = 1280
INNER = 640
KERNEL = 5
DILATION = 64
LENGTH = 1024
STEP = 10
MARGIN = KERNEL // 2 * DILATION
OFFSETS = tuple((k - KERNEL // 2) * DILATION for k in range(KERNEL))
BLOCK = 256
STEPS = LENGTH // BLOCK

NORM_EPS = 1e-05
ADAM_EPS = 1e-08
BETA_ONE = 0.9
BETA_TWO = 0.95
CLIP_LIMIT = 1.0
RATE_MATRIX = 0.04
RATE_VECTOR = 0.3
DECAY_MATRIX = 0.1
GELU_C = 0.7978845608
GELU_K = 0.044715

GAIN_ONE, SHIFT_ONE = (0, 1280), (1280, 1280)
GAIN_TWO, SHIFT_TWO = (2560, 640), (3200, 640)
GAIN_THREE, SHIFT_THREE = (3840, 640), (4480, 640)
BIAS_ONE, BIAS_TWO, BIAS_THREE = (5120, 640), (5760, 640), (6400, 1280)

BF16 = jnp.bfloat16
F32 = jnp.float32
AXES = ("dp", "fsdp")
VMEM_LIMIT = 18 * 1024 * 1024
MIDDLE_LIMIT = 27 * 1024 * 1024
WIDE_LIMIT = 34 * 1024 * 1024
FLOPS_PER_US = 1.15e9
EFFORT = 4


def round16(n):
    return -(-n // 16) * 16


class Geometry:
    def __init__(self, taps, rows, cols):
        self.taps, self.rows, self.cols = taps, rows, cols
        self.height = taps * rows
        self.tiles, self.rest = divmod(cols, 128)
        self.groups = 128 // self.rest if self.rest and 128 % self.rest == 0 else 1
        self.tile_rows = round16(self.height)
        self.rest_rows = round16(-(-self.height // self.groups)) if self.rest else 0
        self.packed = self.tiles * self.tile_rows + self.rest_rows

    def pack(self, value):
        pieces = [value[:, 128 * t : 128 * t + 128] for t in range(self.tiles)]
        more = self.tile_rows - self.height
        if more:
            empty = jnp.zeros((more, 128), value.dtype)
            pieces = [jnp.concatenate([piece, empty], axis=0) for piece in pieces]
        if self.rest:
            rest = value[:, 128 * self.tiles :]
            spare = self.groups * self.rest_rows - self.height
            if spare:
                rest = jnp.concatenate([rest, jnp.zeros((spare, self.rest), value.dtype)], axis=0)
            n = self.rest_rows
            parts = [rest[n * g : n * g + n] for g in range(self.groups)]
            empty = 128 - self.groups * self.rest
            if empty:
                parts.append(jnp.zeros((n, empty), value.dtype))
            pieces.append(jnp.concatenate(parts, axis=1))
        return jnp.concatenate(pieces, axis=0)

    def unpack(self, packed):
        pieces = [
            packed[self.tile_rows * t : self.tile_rows * t + self.height]
            for t in range(self.tiles)
        ]
        if self.rest:
            base = self.tiles * self.tile_rows
            n, w = self.rest_rows, self.rest
            parts = []
            for g in range(self.groups):
                have = min(n, self.height - n * g)
                if have > 0:
                    parts.append(packed[base : base + have, w * g : w * g + w])
            pieces.append(jnp.concatenate(parts, axis=0))
        return jnp.concatenate(pieces, axis=1)


class Network:
    def __init__(self, dp, fsdp, far_first):
        self.dp, self.fsdp = dp, fsdp
        self.half = dp * fsdp // 2
        far = [("f", b) for b in range(fsdp.bit_length() - 2, 0, -1)]
        near = [("f", 0)] if fsdp > 1 else []
        rows = [("d", b) for b in range(dp.bit_length() - 2, 0, -1)]
        if far_first:
            self.order = (far + near + rows, far[::-1] + rows + near)
        else:
            self.order = (
                far[:1] + near + rows + far[1:],
                far[::-1][:1] + rows + near + far[::-1][1:],
            )

    def flip(self, stage, device):
        d, f = divmod(device, self.fsdp)
        kind, bit = self.order[d & 1][stage]
        if kind == "f":
            f ^= 1 << bit
        else:
            d ^= 1 << bit
        return d * self.fsdp + f

    def stage(self, stage):
        return [(i, self.flip(stage, i)) for i in range(self.dp * self.fsdp)]

    def core(self):
        return [(i, i ^ self.fsdp) for i in range(self.dp * self.fsdp)]

    def stages(self):
        return len(self.order[0])

    def slot(self, d, f, me_d, me_f):
        d_bits = jnp.bitwise_xor(me_d, d)
        f_bits = jnp.bitwise_xor(me_f, f)
        total = jnp.int32(0)
        for i, (kind, bit) in enumerate(self.order[d & 1]):
            source = f_bits if kind == "f" else d_bits
            total = total + (jnp.bitwise_and(lax.shift_right_logical(source, bit), 1) << i)
        return total


def call(kernel, name, out_shape, in_specs, out_specs, grid=(), scratch=(), us=1.0, aliases=None, vmem=VMEM_LIMIT):
    return pl.pallas_call(
        kernel,
        name=name,
        grid=grid,
        out_shape=out_shape,
        in_specs=in_specs,
        out_specs=out_specs,
        scratch_shapes=list(scratch),
        input_output_aliases=aliases or {},
        compiler_params=pltpu.CompilerParams(vmem_limit_bytes=vmem),
        cost_estimate=pl.CostEstimate(
            flops=int(EFFORT * us * FLOPS_PER_US), bytes_accessed=0, transcendentals=0
        ),
    )


def whole(shape):
    return pl.BlockSpec(shape, lambda *_: (0,) * len(shape))


def tokens(width, first=0):
    return pl.BlockSpec((BLOCK, width), lambda i: (first + i, 0))


SMEM = pl.BlockSpec(memory_space=pltpu.SMEM)
ANY = pl.BlockSpec(memory_space=pl.ANY)


def shape(dims, dtype):
    return jax.ShapeDtypeStruct(dims, dtype)


def part(vec_ref, span):
    return vec_ref[:, span[0] : span[0] + span[1]]


def add_rows(ref, value):
    ref[...] += jnp.sum(value, axis=0, keepdims=True)


HALF = LENGTH // 2


def for_halves(body, *sums):
    for ref in sums:
        ref[...] = jnp.zeros(ref.shape, ref.dtype)

    @pl.loop(0, 2)
    def _(step):
        body(pl.multiple_of(step * HALF, HALF))


def blocks_of(start):
    return [
        (slice(offset, offset + BLOCK), pl.ds(pl.multiple_of(start + offset, BLOCK), BLOCK))
        for offset in range(0, HALF, BLOCK)
    ]


def for_rows(count, size, loop, body):
    if loop:

        @pl.loop(0, count)
        def _(step):
            body(pl.ds(pl.multiple_of(step * size, size), size))
    else:
        for step in range(count):
            body(slice(step * size, step * size + size))


def statistics(values):
    width = values.shape[1]
    mean = jnp.sum(values, axis=1, keepdims=True) * (1.0 / width)
    center = values - mean
    spread = jnp.sum(center * center, axis=1, keepdims=True) * (1.0 / width)
    return center, lax.rsqrt(spread + NORM_EPS)


def gelu(a):
    t = jnp.tanh(GELU_C * (a + GELU_K * (a * a * a)))
    return 0.5 * a * (1.0 + t)


def gelu_slope(a):
    square = a * a
    t = jnp.tanh(GELU_C * a * (1.0 + GELU_K * square))
    half = 0.5 * (1.0 + t)
    return half + half * (1.0 - t) * a * (GELU_C + (3.0 * GELU_C * GELU_K) * square)


def norm_backward(grad, normed, root, gain, shift):
    width = grad.shape[1]
    d_a = grad * gelu_slope(normed * gain + shift)
    scaled = d_a * gain
    mean_one = jnp.sum(scaled, axis=1, keepdims=True) * (1.0 / width)
    mean_two = jnp.sum(scaled * normed, axis=1, keepdims=True) * (1.0 / width)
    return root * (scaled - mean_one - normed * mean_two), d_a * normed, d_a


def build_taps(ends_ref, source, padded, target, sign):
    width = source.shape[1]
    count = ends_ref.shape[0]
    empty = jnp.zeros((MARGIN, width), BF16)
    padded[0:MARGIN] = empty
    padded[MARGIN : MARGIN + LENGTH] = source[...]
    padded[MARGIN + LENGTH : MARGIN + LENGTH + MARGIN] = empty

    @pl.loop(0, STEPS)
    def _(step):
        start = pl.multiple_of(step * BLOCK, BLOCK)
        position = start + lax.broadcasted_iota(jnp.int32, (BLOCK, 128), 0)
        lower = jnp.zeros((BLOCK, 128), jnp.int32)
        upper = jnp.full((BLOCK, 128), ends_ref[count - 1], jnp.int32)
        for j in range(count - 1):
            lower = jnp.where(position >= ends_ref[j], ends_ref[j], lower)
        for j in range(count - 2, -1, -1):
            upper = jnp.where(position < ends_ref[j], ends_ref[j], upper)
        for k in range(KERNEL):
            offset = sign * OFFSETS[k]
            moved = position + offset
            mask = jnp.where((moved >= lower) & (moved < upper), 1.0, 0.0).astype(BF16)
            mask = jnp.concatenate([mask] * (width // 128), axis=1)
            value = padded[pl.ds(pl.multiple_of(start + MARGIN + offset, DILATION), BLOCK)]
            target[pl.ds(start, BLOCK), k * width : k * width + width] = value * mask


def build_taps_unrolled(ends_ref, source, target, sign):
    width = source.shape[1]
    count = ends_ref.shape[0]
    for rows in (slice(start, start + BLOCK) for start in range(0, LENGTH, BLOCK)):
        position = rows.start + lax.broadcasted_iota(jnp.int32, (BLOCK, 128), 0)
        lower = jnp.zeros((BLOCK, 128), jnp.int32)
        upper = jnp.full((BLOCK, 128), ends_ref[count - 1], jnp.int32)
        for j in range(count - 1):
            lower = jnp.where(position >= ends_ref[j], ends_ref[j], lower)
        for j in range(count - 2, -1, -1):
            upper = jnp.where(position < ends_ref[j], ends_ref[j], upper)
        for k in range(KERNEL):
            offset = sign * OFFSETS[k]
            moved = position + offset
            mask = jnp.where((moved >= lower) & (moved < upper), 1.0, 0.0).astype(BF16)
            mask = jnp.concatenate([mask] * (width // 128), axis=1)
            columns = slice(k * width, k * width + width)
            start = max(rows.start, -offset)
            stop = min(rows.stop, LENGTH - offset)
            value = source[start + offset : stop + offset]
            target[start:stop, columns] = value * mask[start - rows.start : stop - rows.start]
            if rows.start < start:
                target[rows.start : start, columns] = jnp.zeros((start - rows.start, width), BF16)
            if stop < rows.stop:
                target[stop : rows.stop, columns] = jnp.zeros((rows.stop - stop, width), BF16)


def dot(a, b):
    return jnp.dot(a, b, preferred_element_type=F32)


def dot_nt(a, b):
    return lax.dot_general(a, b, (((1,), (1,)), ((), ())), preferred_element_type=F32)


def assemble(net, geo, me_ref, own, peer, buffer, sems, full, beside=None, loop=False):
    core = jnp.bitwise_and(me_ref[0], 1)
    first = pltpu.make_async_copy(own, buffer.at[core], sems.at[0])
    second = pltpu.make_async_copy(peer, buffer.at[1 - core], sems.at[1])
    first.start()
    second.start()
    first.wait()
    second.wait()
    width = net.dp * geo.cols

    def body(f, first_row):
        blocks = [
            geo.unpack(buffer[d & 1, net.slot(d, f, me_ref[0], me_ref[1])])
            for d in range(net.dp)
        ]
        row = jnp.concatenate(blocks, axis=1)
        for k in range(geo.taps):
            value = row[k * geo.rows : k * geo.rows + geo.rows]
            full[pl.ds(k * geo.rows * net.fsdp + first_row, geo.rows)] = value
            if beside is not None:
                beside[pl.ds(first_row, geo.rows), k * width : k * width + width] = value

    if loop and geo.rows % 16 == 0:

        @pl.loop(0, net.fsdp)
        def _(f):
            body(f, pl.multiple_of(f * geo.rows, 16))
    else:
        for f in range(net.fsdp):
            body(f, f * geo.rows)


def distribute(net, geo, me_ref, full, buffer, sems, keep, send):
    width = net.dp * geo.cols
    for f in range(net.fsdp):
        pieces = [
            full[f * geo.rows : f * geo.rows + geo.rows, k * width : k * width + width]
            for k in range(geo.taps)
        ]
        row = pieces[0] if geo.taps == 1 else jnp.concatenate(pieces, axis=0)
        for d in range(net.dp):
            buffer[d & 1, net.slot(d, f, me_ref[0], me_ref[1])] = geo.pack(
                row[:, d * geo.cols : d * geo.cols + geo.cols]
            )
    core = jnp.bitwise_and(me_ref[0], 1)
    first = pltpu.make_async_copy(buffer.at[1 - core], send, sems.at[0])
    second = pltpu.make_async_copy(buffer.at[core], keep, sems.at[1])
    first.start()
    second.start()
    first.wait()
    second.wait()


def slots(net, geo):
    return (net.half, geo.packed, 128)


def piece_scratch(net, geo):
    return [pltpu.VMEM((2,) + slots(net, geo), BF16), pltpu.SemaphoreType.DMA((2,))]


def pack_weights(geos, *weights):
    rows = sum(geo.packed for geo in geos)

    def kernel(*refs):
        start = 0
        for geo, source in zip(geos, refs):
            refs[-1][start : start + geo.packed] = geo.pack(source[...].astype(BF16))
            start += geo.packed

    return call(
        kernel,
        "pack_weights",
        shape((rows, 128), BF16),
        [whole(w.shape) for w in weights],
        whole((rows, 128)),
        us=1.0,
    )(*weights)


def first_norm(block_input, cotangent, vec, first, held=()):
    def kernel(x_ref, cot_ref, vec_ref, *refs):
        h_ref, ht_ref, stat_ref, bias_ref = refs[-4:]

        def body(rows):
            values = x_ref[rows].astype(F32)
            center, root = statistics(values)
            normed = center * root
            hidden = gelu(normed * part(vec_ref, GAIN_ONE) + part(vec_ref, SHIFT_ONE)).astype(BF16)
            h_ref[rows] = hidden
            ht_ref[:, rows] = hidden.T
            lane = lax.broadcasted_iota(jnp.int32, (BLOCK // 2, 128), 1)
            stat_ref[rows] = jnp.where(lane == 0, values[:, :1] - center[:, :1], root)
            bias_ref[...] += jnp.sum(cot_ref[rows].astype(F32), axis=0, keepdims=True)

        @pl.when(pl.program_id(0) == 0)
        def _():
            bias_ref[...] = jnp.zeros((1, D), F32)

        for_rows(2, BLOCK // 2, True, body)

    return call(
        kernel,
        "first_norm",
        [
            shape((LENGTH, D), BF16),
            shape((D, LENGTH), BF16),
            shape((LENGTH, 128), F32),
            shape((1, D), F32),
        ],
        [tokens(D, first), tokens(D, first), whole(vec.shape)] + [ANY] * len(held),
        [
            tokens(D, first),
            pl.BlockSpec((D, BLOCK), lambda i: (0, first + i)),
            tokens(128, first),
            whole((1, D)),
        ],
        grid=(2,),
        aliases={3 + i: i for i in range(len(held))},
        us=2.8,
    )(block_input, cotangent, vec, *held)


def norm_out(rows, mixed, vec_ref, gain, shift_span, h_ref, ht_ref, normed_ref, root_ref):
    center, root = statistics(mixed)
    normed = center * root
    hidden = gelu(normed * part(vec_ref, gain) + part(vec_ref, shift_span)).astype(BF16)
    h_ref[rows] = hidden
    ht_ref[:, rows] = hidden.T
    normed_ref[rows] = normed
    root_ref[rows] = jnp.broadcast_to(root, (root.shape[0], 128))


NORM_SHAPES = [
    shape((LENGTH, INNER), BF16),
    shape((INNER, LENGTH), BF16),
    shape((LENGTH, INNER), F32),
    shape((LENGTH, 128), F32),
]


def wholes(shapes):
    return [whole(s.shape) for s in shapes]


def mix_one(net, geo, me, own, peer, hidden_one, vec):
    def kernel(me_ref, own_ref, peer_ref, h1_ref, vec_ref, h_ref, ht_ref, n_ref, r_ref, full, buf, sems):
        assemble(net, geo, me_ref, own_ref, peer_ref, buf, sems, full, loop=True)

        def body(rows):
            mixed = dot(h1_ref[rows], full[...]) + part(vec_ref, BIAS_ONE)
            norm_out(rows, mixed, vec_ref, GAIN_TWO, SHIFT_TWO, h_ref, ht_ref, n_ref, r_ref)

        for_rows(2 * STEPS, BLOCK // 2, True, body)

    outs = NORM_SHAPES + [shape((D, INNER), BF16)]
    return call(
        kernel,
        "mix_one",
        outs,
        [SMEM, ANY, ANY, whole((LENGTH, D)), whole(vec.shape)],
        wholes(outs),
        scratch=piece_scratch(net, geo),
        us=0.01,
    )(me, own, peer, hidden_one, vec)


def mix_two(net, geo, me, ends, own, peer, hidden_two, vec):
    def kernel(
        me_ref, ends_ref, own_ref, peer_ref, h2_ref, vec_ref, h_ref, ht_ref, n_ref, r_ref, beside, full, buf, sems, taps
    ):
        assemble(net, geo, me_ref, own_ref, peer_ref, buf, sems, full, beside)
        build_taps_unrolled(ends_ref, h2_ref, taps, 1)
        n_ref[...] = dot(taps[...], full[...])

        def body(rows):
            mixed = n_ref[rows] + part(vec_ref, BIAS_TWO)
            norm_out(rows, mixed, vec_ref, GAIN_THREE, SHIFT_THREE, h_ref, ht_ref, n_ref, r_ref)

        for_rows(STEPS, BLOCK, False, body)

    outs = NORM_SHAPES + [shape((INNER, KERNEL * INNER), BF16)]
    return call(
        kernel,
        "mix_two",
        outs,
        [SMEM, SMEM, ANY, ANY, whole((LENGTH, INNER)), whole(vec.shape)],
        wholes(outs),
        scratch=[pltpu.VMEM((KERNEL * INNER, INNER), BF16)]
        + piece_scratch(net, geo)
        + [
            pltpu.VMEM((LENGTH, KERNEL * INNER), BF16),
        ],
        us=11.7,
        vmem=WIDE_LIMIT,
    )(me, ends, own, peer, hidden_two, vec)


def norm_in(product, vec_ref, gain, shift_span, grad, n_ref, r_ref, back_ref, *sums):
    def body(start):
        grad[...] = product(pl.ds(start, HALF))
        for part_rows, rows in blocks_of(start):
            back, to_gain, to_shift = norm_backward(
                grad[part_rows],
                n_ref[rows],
                r_ref[rows][:, :1],
                part(vec_ref, gain),
                part(vec_ref, shift_span),
            )
            back = back.astype(BF16)
            back_ref[rows] = back
            for ref, value in zip(sums, (to_gain, to_shift, back.astype(F32))):
                add_rows(ref, value)

    for_halves(body, *sums)


def gradient_shapes(net, geo):
    return [shape(slots(net, geo), BF16)] * 2


def weight_gradient(net, geo, me, left, right, name="weight_gradient"):
    dims = (left.shape[0], right.shape[1])

    def kernel(me_ref, left_ref, right_ref, keep, send, full, buf, sems):
        full[...] = dot(left_ref[...], right_ref[...]).astype(BF16)
        distribute(net, geo, me_ref, full, buf, sems, keep, send)

    return call(
        kernel,
        name,
        gradient_shapes(net, geo),
        [SMEM, whole(left.shape), whole(right.shape)],
        [ANY, ANY],
        scratch=[pltpu.VMEM(dims, BF16)] + piece_scratch(net, geo),
        us=3.0 if dims[0] < dims[1] else 3.7,
    )(me, left, right)


def back_through_out(net, geo, me, own, peer, cotangent, normed, root, vec):
    def kernel(
        me_ref, own_ref, peer_ref, cot_ref, n_ref, r_ref, vec_ref, back_ref, gg_ref, gs_ref, gb_ref, full, buf, sems, grad
    ):
        assemble(net, geo, me_ref, own_ref, peer_ref, buf, sems, full)

        def product(rows):
            return dot_nt(cot_ref[rows], full[...])

        norm_in(product, vec_ref, GAIN_THREE, SHIFT_THREE, grad, n_ref, r_ref, back_ref, gg_ref, gs_ref, gb_ref)

    row = shape((1, INNER), F32)
    outs = [shape((LENGTH, INNER), BF16), row, row, row, shape((INNER, D), BF16)]
    return call(
        kernel,
        "back_through_out",
        outs,
        [SMEM, ANY, ANY] + wholes((cotangent, normed, root, vec)),
        wholes(outs),
        scratch=piece_scratch(net, geo) + [pltpu.VMEM((HALF, INNER), F32)],
        us=6.4,
    )(me, own, peer, cotangent, normed, root, vec)


def block_result(block_input, hidden_three, full_out, vec):
    half = LENGTH // 2

    def kernel(x_ref, h_ref, w_ref, vec_ref, out_ref):
        branch = dot(h_ref[...], w_ref[...]) + part(vec_ref, BIAS_THREE)
        out_ref[...] = (x_ref[...].astype(F32) + branch).astype(BF16)

    def rows_of(width):
        return pl.BlockSpec((half, width), lambda i: (i, 0))

    return call(
        kernel,
        "block_result",
        shape((LENGTH, D), BF16),
        [rows_of(D), rows_of(INNER), whole((INNER, D)), whole(vec.shape)],
        rows_of(D),
        grid=(2,),
        us=3.8,
    )(block_input, hidden_three, full_out, vec)


def conv_gradient(net, geo, me, ends, hidden_two_t, back_two):
    step = 2 * INNER
    width = KERNEL * INNER

    def kernel(me_ref, ends_ref, left_ref, back_ref, keep, send, taps, full, buf, sems, pad):
        build_taps(ends_ref, back_ref, pad, taps, -1)
        for start in range(0, width, step):
            columns = slice(start, min(start + step, width))
            full[:, columns] = dot(left_ref[...], taps[:, columns]).astype(BF16)
        distribute(net, geo, me_ref, full, buf, sems, keep, send)

    outs = gradient_shapes(net, geo) + [shape((LENGTH, width), BF16)]
    return call(
        kernel,
        "conv_gradient",
        outs,
        [SMEM, SMEM, whole((INNER, LENGTH)), whole((LENGTH, INNER))],
        [ANY, ANY, whole((LENGTH, width))],
        scratch=[pltpu.VMEM((INNER, width), BF16)]
        + piece_scratch(net, geo)
        + [pltpu.VMEM((LENGTH + 2 * MARGIN, INNER), BF16)],
        us=8.0,
        vmem=MIDDLE_LIMIT,
    )(me, ends, hidden_two_t, back_two)


def back_through_conv(taps, full_conv, normed, root, vec):
    def kernel(taps_ref, w_ref, n_ref, r_ref, vec_ref, back_ref, gg_ref, gs_ref, gb_ref, grad):
        def product(rows):
            return dot_nt(taps_ref[rows], w_ref[...])

        norm_in(product, vec_ref, GAIN_TWO, SHIFT_TWO, grad, n_ref, r_ref, back_ref, gg_ref, gs_ref, gb_ref)

    row = shape((1, INNER), F32)
    outs = [shape((LENGTH, INNER), BF16), row, row, row]
    return call(
        kernel,
        "back_through_conv",
        outs,
        wholes((taps, full_conv, normed, root, vec)),
        wholes(outs),
        scratch=[pltpu.VMEM((HALF, INNER), F32)],
        us=10.0,
    )(taps, full_conv, normed, root, vec)


def back_through_in(back_one, full_in, block_input, cotangent, stat, vec):
    def kernel(back_ref, w_ref, x_ref, cot_ref, stat_ref, vec_ref, out_ref, gg_ref, gs_ref, grad):
        @pl.when(pl.program_id(0) == 0)
        def _():
            gg_ref[...] = jnp.zeros((1, D), F32)
            gs_ref[...] = jnp.zeros((1, D), F32)

        grad[...] = dot_nt(back_ref[...], w_ref[...])
        for start in range(0, HALF, BLOCK):
            rows = slice(start, start + BLOCK)
            root = stat_ref[rows, 1:2]
            normed = (x_ref[rows].astype(F32) - stat_ref[rows, :1]) * root
            back, to_gain, to_shift = norm_backward(
                grad[rows], normed, root, part(vec_ref, GAIN_ONE), part(vec_ref, SHIFT_ONE)
            )
            out_ref[rows] = (cot_ref[rows].astype(F32) + back).astype(BF16)
            add_rows(gg_ref, to_gain)
            add_rows(gs_ref, to_shift)

    def rows_of(width):
        return pl.BlockSpec((HALF, width), lambda i: (i, 0))

    row = shape((1, D), F32)
    return call(
        kernel,
        "back_through_in",
        [shape((LENGTH, D), BF16), row, row],
        [rows_of(INNER), whole((D, INNER)), rows_of(D), rows_of(D), rows_of(128), whole(vec.shape)],
        [rows_of(D)] + [whole((1, D))] * 2,
        grid=(2,),
        scratch=[pltpu.VMEM((HALF, D), F32)],
        us=9.4,
    )(back_one, full_in, block_input, cotangent, stat, vec)


def sum_squares(owned, pieces):
    rows = sum(piece.shape[1] for piece in pieces) // 128
    total_rows = -(-(rows + 1) // 8) * 8
    n = len(owned)

    def kernel(*refs):
        out = refs[-1]
        total = jnp.zeros((1, 128), F32)
        for ref in refs[:n]:
            value = ref[...]
            total = total + jnp.sum(value * value, axis=0, keepdims=True)
        out[...] = jnp.zeros(out.shape, F32)
        row = 0
        for ref in refs[n:-1]:
            for start in range(0, ref.shape[1], 128):
                out[row : row + 1] = ref[:, start : start + 128]
                row += 1
        out[rows : rows + 1] = total

    return call(
        kernel,
        "sum_squares",
        shape((total_rows, 128), F32),
        [whole(v.shape) for v in (*owned, *pieces)],
        whole((total_rows, 128)),
        us=0.3,
    )(*owned, *pieces)


def adamw(weight, moment, square, gradient, rate, decay):
    new_moment = BETA_ONE * moment + (1.0 - BETA_ONE) * gradient
    new_square = BETA_TWO * square + (1.0 - BETA_TWO) * gradient * gradient
    moment_hat = new_moment * (1.0 / (1.0 - BETA_ONE**STEP))
    square_hat = new_square * (1.0 / (1.0 - BETA_TWO**STEP))
    update = moment_hat / (jnp.sqrt(square_hat) + ADAM_EPS)
    return weight - rate * (update + decay * weight), new_moment, new_square


def update_all(geos, owned, totals, weights, vectors):
    n = len(geos)
    size = vectors[0].shape[0]

    def kernel(*refs):
        owned_refs, total_ref = refs[:n], refs[n]
        ins = refs[n + 1 : n + 1 + 3 * n + 3]
        outs, held = refs[n + 1 + 3 * n + 3 : -1], refs[-1]

        def update(i, rows, gradient):
            weight, moment, square = (r[rows] for r in ins[3 * i : 3 * i + 3])
            results = adamw(weight, moment, square, gradient, RATE_MATRIX, DECAY_MATRIX)
            for ref, value in zip(outs[1 + 3 * i : 4 + 3 * i], results):
                ref[rows] = value

        grad_vec = total_ref[0:size]
        squares = jnp.sum(grad_vec * grad_vec, axis=0, keepdims=True) + total_ref[size : size + 1]
        norm = jnp.sqrt(jnp.sum(squares, axis=1, keepdims=True))
        outs[0][...] = norm
        clip = jnp.minimum(1.0, CLIP_LIMIT / (norm + 1e-06))
        for i, geo in enumerate(geos):
            gradient = geo.unpack(owned_refs[i][...].astype(F32)) * clip
            if geo.taps == 1 or geo.rows % 8:
                update(i, slice(None), gradient)
            else:
                held[...] = gradient

                @pl.loop(0, geo.taps)
                def _(k):
                    rows = pl.ds(pl.multiple_of(k * geo.rows, 8), geo.rows)
                    update(i, rows, held[rows])

        weight, moment, square = (r[...] for r in ins[3 * n :])
        results = adamw(weight, moment, square, grad_vec * clip, RATE_VECTOR, 0.0)
        for ref, value in zip(outs[1 + 3 * n :], results):
            ref[...] = value

    args = list(owned) + [totals] + [v for group in weights for v in group] + list(vectors)
    outs = [shape((1, 1), F32)]
    outs += [shape(v.shape, F32) for group in weights for v in group]
    outs += [shape(v.shape, F32) for v in vectors]
    return call(
        kernel,
        "update_all",
        outs,
        [whole(v.shape) for v in args],
        [whole(o.shape) for o in outs],
        scratch=[pltpu.VMEM(weights[1][0].shape, F32)],
        us=2.0,
    )(*args)


class Sequence:
    def __init__(self):
        self.last = ()

    def after(self, *values):
        return lax.optimization_barrier(tuple(values) + self.last)[: len(values)]

    def run(self, function, *values, **options):
        result = function(*self.after(*values), **options)
        self.last = tuple(jax.tree.leaves(result))[-1:]
        return result

    def wait(self, *values):
        self.last = tuple(values) + self.last


class Gather:
    def __init__(self, net, seq, shard):
        self.net, self.seq, self.stage = net, seq, 0
        self.held, self.coming = shard[None], None

    def send(self):
        (held,) = self.seq.after(self.held)
        self.held = held
        last = self.stage == self.net.stages()
        self.coming = lax.ppermute(held, AXES, self.net.core() if last else self.net.stage(self.stage))
        self.stage += 1

    def take(self):
        self.held, self.coming = self.seq.after(self.held, self.coming)
        if self.stage <= self.net.stages():
            self.held = jnp.concatenate([self.held, self.coming], axis=0)
        self.seq.wait(self.held, self.coming)

    def step(self):
        self.take()
        self.send()

    def finish(self):
        while self.stage <= self.net.stages():
            self.step()
        self.take()


def add(a, b):
    return (a.astype(F32) + b.astype(F32)).astype(BF16)


class Reduce:
    def __init__(self, net, seq, keep, send):
        self.net, self.seq, self.stage = net, seq, net.stages()
        self.keep = keep
        (send,) = seq.after(send)
        self.coming = lax.ppermute(send, AXES, net.core())

    def step(self):
        self.stage -= 1
        self.keep, self.coming = self.seq.after(self.keep, self.coming)
        half = self.keep.shape[0] // 2
        away = add(self.keep[half:], self.coming[half:])
        keep = add(self.keep[:half], self.coming[:half])
        self.keep, away = self.seq.after(keep, away)
        self.seq.wait(self.keep, away)
        self.coming = lax.ppermute(away, AXES, self.net.stage(self.stage))

    def end(self):
        while self.stage:
            self.step()
        self.keep, self.coming = self.seq.after(self.keep, self.coming)
        held = self.keep.astype(F32) + self.coming.astype(F32)
        self.seq.wait(held)
        return held[0]


def total_sum(net, value):
    value = value + lax.ppermute(value, AXES, net.core())
    for stage in range(net.stages()):
        value = value + lax.ppermute(value, AXES, net.stage(stage))
    return value


def body(
    dp,
    fsdp,
    block_input,
    cotangent,
    protein_lengths,
    weight_in,
    moment_in,
    square_in,
    weight_conv,
    moment_conv,
    square_conv,
    weight_out,
    moment_out,
    square_out,
    vectors,
    moment_vectors,
    square_vectors,
):
    net = Network(dp, fsdp, True)
    net_ends = Network(dp, fsdp, False)
    geo_in = Geometry(1, weight_in.shape[0], weight_in.shape[1])
    geo_conv = Geometry(KERNEL, weight_conv.shape[1], weight_conv.shape[2])
    geo_out = Geometry(1, weight_out.shape[0], weight_out.shape[1])
    geos = (geo_in, geo_conv, geo_out)

    def flat(v):
        return v.reshape(-1, v.shape[-1])

    me = jnp.stack([lax.axis_index("dp"), lax.axis_index("fsdp")]).astype(jnp.int32)
    ends = jnp.cumsum(protein_lengths[0]).astype(jnp.int32)
    vec = vectors.reshape(1, -1)
    x = block_input[0]
    cot = cotangent[0]

    seq = Sequence()
    shard_in = seq.run(functools.partial(pack_weights, (geo_in,)), weight_in)
    get_in = Gather(net_ends, seq, shard_in)
    get_in.send()
    shard_conv = seq.run(functools.partial(pack_weights, (geo_conv,)), flat(weight_conv))
    get_conv = Gather(net, seq, shard_conv)
    get_conv.send()
    shard_out = seq.run(functools.partial(pack_weights, (geo_out,)), weight_out)
    get_out = Gather(net, seq, shard_out)
    seq.wait(me, ends, vec)
    norms = seq.run(first_norm, x, cot, vec, first=0)
    get_in.step()
    get_conv.step()
    get_out.send()
    h1, h1_t, stat, half_b3 = seq.run(
        lambda x, cot, vec, *held: first_norm(x, cot, vec, STEPS // 2, held), x, cot, vec, *norms[:3]
    )
    grad_b3 = norms[3] + half_b3
    get_in.step()
    get_conv.step()
    get_out.step()
    get_in.step()
    get_conv.step()
    get_in.finish()
    h2, h2_t, n2, r2, full_in = seq.run(
        functools.partial(mix_one, net_ends, geo_in), me, get_in.held, get_in.coming, h1, vec
    )
    get_out.step()
    get_conv.step()
    get_conv.finish()
    get_out.step()
    h3, h3_t, n3, r3, full_conv = seq.run(
        functools.partial(mix_two, net, geo_conv),
        me, ends, get_conv.held, get_conv.coming, h2, vec,
    )
    get_out.step()
    pieces = seq.run(
        functools.partial(weight_gradient, net_ends, geo_out, name="out_gradient"), me, h3_t, cot
    )
    sum_out = Reduce(net_ends, seq, *pieces)
    get_out.finish()
    back_two, grad_g3, grad_s3, grad_b2, full_out = seq.run(
        functools.partial(back_through_out, net, geo_out),
        me, get_out.held, get_out.coming, cot, n3, r3, vec,
    )
    sum_out.step()
    keep, send, taps = seq.run(
        functools.partial(conv_gradient, net, geo_conv), me, ends, h2_t, back_two
    )
    sum_conv = Reduce(net, seq, keep, send)
    back_one, grad_g2, grad_s2, grad_b1 = seq.run(
        back_through_conv, taps, full_conv, n2, r2, vec
    )
    sum_conv.step()
    sum_out.step()
    pieces = seq.run(
        functools.partial(weight_gradient, net_ends, geo_in, name="in_gradient"),
        me, h1_t, back_one,
    )
    sum_in = Reduce(net_ends, seq, *pieces)
    block_output = seq.run(block_result, x, h3, full_out, vec)
    sum_in.step()
    sum_conv.step()
    sum_out.step()
    input_grad, grad_g1, grad_s1 = seq.run(
        back_through_in, back_one, full_in, x, cot, stat, vec
    )
    sum_in.step()
    sum_conv.step()
    sum_out.step()
    sum_in.step()
    sum_conv.step()
    grad_out = sum_out.end()
    sum_in.step()
    grad_conv = sum_conv.end()
    grad_in = sum_in.end()

    owned = (grad_in, grad_conv, grad_out)
    pieces = (grad_g1, grad_s1, grad_g2, grad_s2, grad_g3, grad_s3, grad_b1, grad_b2, grad_b3)
    totals = total_sum(net, sum_squares(owned, pieces))
    results = update_all(
        geos,
        owned,
        totals,
        (
            (weight_in, moment_in, square_in),
            (flat(weight_conv), flat(moment_conv), flat(square_conv)),
            (weight_out, moment_out, square_out),
        ),
        tuple(v.reshape(-1, 128) for v in (vectors, moment_vectors, square_vectors)),
    )
    norm, news = results[0], results[1:]
    return (
        block_output[None],
        input_grad[None],
        norm[0, 0],
        *news[0:3],
        *(v.reshape(weight_conv.shape) for v in news[3:6]),
        *news[6:9],
        *(v.reshape(-1) for v in news[9:12]),
    )


def solution(mesh):
    rows = P(("dp", "fsdp"), None, None)
    matrix = P("fsdp", "dp")
    taps = P(None, "fsdp", "dp")
    weights = (matrix,) * 3 + (taps,) * 3 + (matrix,) * 3 + (P(),) * 3
    return jax.shard_map(
        functools.partial(body, mesh.shape["dp"], mesh.shape["fsdp"]),
        mesh=mesh,
        in_specs=(rows, rows, P(("dp", "fsdp"), None)) + weights,
        out_specs=(rows, rows, P()) + weights,
        check_vma=False,
    )
```

profile of v0, /device:TPU:0, one launch (start us, length us, event | category | flops | bytes accessed | tf_op | source)
XLA Modules:
  0.0 167.4 jit_solution(18058115167191614419)
XLA Ops:
  0.7 1.0 copy-done.9
  1.7 4.1 %collective-permute-start.1 = (bf16[1,208,128]{2,1,0:T(8,128)(2,1)S(1)}, bf16[1,208,128]{2,1,0:T(8,128)(2,1)}, u32[]{:S(2)}, u32[]{:S(2)}) collective-permute-start(bf16[1,208,128]{2,1,0:T(8,128)(2,1)S(1)} %bitcast.34), channel_id=1, source_target_pairs={{0,4},{1,5},{2,6},{3,7},{4,0},{5,1},{6,2},{7,3},{8,10},{9,11},{10,... | collective-permute-start | bytes 159752 | tf_op jit(solution)/shard_map/ppermute | solution.py:782
  6.0 0.6 copy-done
  6.9 0.5 copy-done.25
  7.4 0.2 reduce-window.9
  7.5 0.9 copy-done.2
  8.5 1.7 %copy-done.3 = bf16[1,1024,1280]{2,1,0:T(8,128)(2,1)S(1)} copy-done((bf16[1,1024,1280]{2,1,0:T(8,128)(2,1)S(1)}, bf16[1,1024,1280]{2,1,0:T(8,128)(2,1)}, u32[]{:S(2)}) %copy-start.3) | copy-done | bytes 2621464
  10.2 2.8 %first_norm.2 = (bf16[1024,1280]{1,0:T(8,128)(2,1)S(1)}, bf16[1280,1024]{1,0:T(8,128)(2,1)S(1)}, f32[1024,128]{1,0:T(8,128)S(1)}, f32[1,1280]{1,0:T(1,128)S(1)}) custom-call(bf16[1024,1280]{1,0:T(8,128)(2,1)S(1)} %bitcast.37, bf16[1024,1280]{1,0:T(8,128)(2,1)S(1)} %bitcast.41, f32[1,7680]{1,0:T(1,128)S(1)} %reshape.100.vec_ref), custom_call_target="tpu_custom_call" | custom-call | flops 12880000000 | tf_op jit(solution)/shard_map/first_norm/pallas_call | solution.py:403
  13.0 0.8 constant_dynamic-update-slice_fusion
  13.9 1.6 collective-permute-start.3
  15.5 2.3 %collective-permute-start.6 = (bf16[1,208,128]{2,1,0:T(8,128)(2,1)S(1)}, bf16[1,208,128]{2,1,0:T(8,128)(2,1)S(1)}, u32[]{:S(2)}, u32[]{:S(2)}) collective-permute-start(bf16[1,208,128]{2,1,0:T(8,128)(2,1)S(1)} %bitcast.32), channel_id=1, source_target_pairs={{0,4},{1,5},{2,6},{3,7},{4,0},{5,1},{6,2},{7,3},{8,10},{9,11},{10,... | collective-permute-start | bytes 159752 | tf_op jit(solution)/shard_map/ppermute | solution.py:782
  17.7 1.6 collective-permute-start.2
  19.3 2.8 %first_norm.3 = (bf16[1024,1280]{1,0:T(8,128)(2,1)S(1)}, bf16[1280,1024]{1,0:T(8,128)(2,1)S(1)}, f32[1024,128]{1,0:T(8,128)S(1)}, f32[1,1280]{1,0:T(1,128)S(1)}) custom-call(bf16[1024,1280]{1,0:T(8,128)(2,1)S(1)} %bitcast.38, bf16[1024,1280]{1,0:T(8,128)(2,1)S(1)} %bitcast.42, ...), custom_call_target="tpu_custom_call", output_to_operand_aliasing={{0}: (3, {}), {1}: (4, {}), {2}: (5, {})} | custom-call | flops 12880000000 | tf_op jit(solution)/shard_map/first_norm/pallas_call | solution.py:403
  22.2 1.6 collective-permute-start.5
  23.8 2.6 %collective-permute-done.2 = bf16[2,512,128]{2,1,0:T(8,128)(2,1)S(1)} collective-permute-done((bf16[2,512,128]{2,1,0:T(8,128)(2,1)S(1)}, bf16[2,512,128]{2,1,0:T(8,128)(2,1)S(1)}, u32[]{:S(2)}, u32[]{:S(2)}) %collective-permute-start.2) | collective-permute-done | bytes 262176 | tf_op jit(solution)/shard_map/ppermute | solution.py:782
  26.5 0.6 collective-permute-start.4
  27.2 1.7 %collective-permute-done.5 = bf16[4,208,128]{2,1,0:T(8,128)(2,1)S(1)} collective-permute-done((bf16[4,208,128]{2,1,0:T(8,128)(2,1)S(1)}, bf16[4,208,128]{2,1,0:T(8,128)(2,1)S(1)}, u32[]{:S(2)}, u32[]{:S(2)}) %collective-permute-start.5) | collective-permute-done | bytes 213024 | tf_op jit(solution)/shard_map/ppermute | solution.py:782
  28.9 0.5 collective-permute-start.9
  29.4 6.3 %collective-permute-done.4 = bf16[4,512,128]{2,1,0:T(8,128)(2,1)S(1)} collective-permute-done((bf16[4,512,128]{2,1,0:T(8,128)(2,1)S(1)}, bf16[4,512,128]{2,1,0:T(8,128)(2,1)S(1)}, u32[]{:S(2)}, u32[]{:S(2)}) %collective-permute-start.4) | collective-permute-done | bytes 524320 | tf_op jit(solution)/shard_map/ppermute | solution.py:782
  35.9 5.3 %collective-permute-done.9 = bf16[8,208,128]{2,1,0:T(8,128)(2,1)S(1)} collective-permute-done((bf16[8,208,128]{2,1,0:T(8,128)(2,1)S(1)}, bf16[8,208,128]{2,1,0:T(8,128)(2,1)S(1)}, u32[]{:S(2)}, u32[]{:S(2)}) %collective-permute-start.9) | collective-permute-done | bytes 426016 | tf_op jit(solution)/shard_map/ppermute | solution.py:782
  41.4 2.5 %collective-permute-start.7 = (bf16[8,512,128]{2,1,0:T(8,128)(2,1)S(1)}, bf16[8,512,128]{2,1,0:T(8,128)(2,1)S(1)}, u32[]{:S(2)}, u32[]{:S(2)}) collective-permute-start(bf16[8,512,128]{2,1,0:T(8,128)(2,1)S(1)} %constant_dynamic-update-slice_fusion.12), channel_id=1, source_target_pairs={{0,16},{1,17},{2,18},{3,19},{4,20},{5,21},{6,22},{7,23},{8,9},{9,8... | collective-permute-start | bytes 3145736 | tf_op jit(solution)/shard_map/ppermute | solution.py:782
  43.9 8.5 %mix_one.1 = (bf16[1024,640]{1,0:T(8,128)(2,1)S(1)}, bf16[640,1024]{1,0:T(8,128)(2,1)S(1)}, f32[1024,640]{1,0:T(8,128)S(1)}, f32[1024,128]{1,0:T(8,128)S(1)}, bf16[1280,640]{1,0:T(8,128)(2,1)S(1)}) custom-call(s32[2]{0:T(128)S(1)} %pad_add_fusion.me_ref, bf16[16,208,128]{2,1,0:T(8,128)(2,1)S(1)} %constant_dynamic-update-slice_fusion.14.own_ref, ...), custom_call_target="tpu_custom_call" | custom-call | flops 46000000 | tf_op jit(solution)/shard_map/mix_one/pallas_call | solution.py:458
  52.5 4.2 %collective-permute-done.7 = bf16[8,512,128]{2,1,0:T(8,128)(2,1)S(1)} collective-permute-done((bf16[8,512,128]{2,1,0:T(8,128)(2,1)S(1)}, bf16[8,512,128]{2,1,0:T(8,128)(2,1)S(1)}, u32[]{:S(2)}, u32[]{:S(2)}) %collective-permute-start.7) | collective-permute-done | bytes 1048608 | tf_op jit(solution)/shard_map/ppermute | solution.py:782
  56.8 0.1 constant_dynamic-update-slice_fusion.18.own_ref
  57.1 4.1 %collective-permute-done.11.peer_ref = bf16[16,512,128]{2,1,0:T(8,128)(2,1)S(1)} collective-permute-done((bf16[16,512,128]{2,1,0:T(8,128)(2,1)S(1)}, bf16[16,512,128]{2,1,0:T(8,128)(2,1)S(1)}, u32[]{:S(2)}, u32[]{:S(2)}) %collective-permute-start.11) | collective-permute-done | bytes 2097184 | tf_op jit(solution)/shard_map/ppermute | solution.py:782
  61.2 1.8 %collective-permute-done.12 = bf16[4,208,128]{2,1,0:T(8,128)(2,1)S(1)} collective-permute-done((bf16[4,208,128]{2,1,0:T(8,128)(2,1)S(1)}, bf16[4,208,128]{2,1,0:T(8,128)(2,1)S(1)}, u32[]{:S(2)}, u32[]{:S(2)}) %collective-permute-start.12) | collective-permute-done | bytes 213024 | tf_op jit(solution)/shard_map/ppermute | solution.py:782
  63.0 2.1 %collective-permute-start.13 = (bf16[8,208,128]{2,1,0:T(8,128)(2,1)S(1)}, bf16[8,208,128]{2,1,0:T(8,128)(2,1)S(1)}, u32[]{:S(2)}, u32[]{:S(2)}) collective-permute-start(bf16[8,208,128]{2,1,0:T(8,128)(2,1)S(1)} %constant_dynamic-update-slice_fusion.20), channel_id=1, source_target_pairs={{0,16},{1,17},{2,18},{3,19},{4,20},{5,21},{6,22},{7,23},{8,9},{9,8... | collective-permute-start | bytes 1277960 | tf_op jit(solution)/shard_map/ppermute | solution.py:782
  65.1 8.8 %mix_two.1 = (bf16[1024,640]{1,0:T(8,128)(2,1)S(1)}, bf16[640,1024]{1,0:T(8,128)(2,1)S(1)}, f32[1024,640]{1,0:T(8,128)S(1)}, f32[1024,128]{1,0:T(8,128)S(1)}, bf16[640,3200]{1,0:T(8,128)(2,1)S(1)}) custom-call(s32[2]{0:T(128)S(1)} %pad_add_fusion.me_ref, s32[4]{0:T(128)S(1)} %bitcast.52, ...), custom_call_target="tpu_custom_call" | custom-call | flops 53819998208 | tf_op jit(solution)/shard_map/mix_two/pallas_call | solution.py:484
  74.0 3.0 %out_gradient.1 = (bf16[16,208,128]{2,1,0:T(8,128)(2,1)S(1)}, bf16[16,208,128]{2,1,0:T(8,128)(2,1)S(1)}) custom-call(s32[2]{0:T(128)S(1)} %pad_add_fusion.me_ref, bf16[640,1024]{1,0:T(8,128)(2,1)S(1)} %get-tuple-element.298.left_ref, bf16[1024,1280]{1,0:T(8,128)(2,1)S(1)} %bitcast.43), custom_call_target="tpu_custom_call" | custom-call | flops 13799999488 | tf_op jit(solution)/shard_map/out_gradient/pallas_call | solution.py:530
  77.1 0.6 collective-permute-start.15
  77.6 6.1 %back_through_out.1 = (bf16[1024,640]{1,0:T(8,128)(2,1)S(1)}, f32[1,640]{1,0:T(1,128)S(1)}, f32[1,640]{1,0:T(1,128)S(1)}, f32[1,640]{1,0:T(1,128)S(1)}, bf16[640,1280]{1,0:T(8,128)(2,1)S(1)}) custom-call(s32[2]{0:T(128)S(1)} %pad_add_fusion.me_ref, bf16[16,208,128]{2,1,0:T(8,128)(2,1)S(1)} %constant_dynamic-update-slice_fusion.22.own_ref, ...), custom_call_target="tpu_custom_call" | custom-call | flops 29440000000 | tf_op jit(solution)/shard_map/back_through_out/pallas_call | solution.py:554
  83.7 0.2 add_convert_fusion.6
  84.0 8.2 %conv_gradient.1 = (bf16[16,512,128]{2,1,0:T(8,128)(2,1)S(1)}, bf16[16,512,128]{2,1,0:T(8,128)(2,1)S(1)}, bf16[1024,3200]{1,0:T(8,128)(2,1)S(1)}) custom-call(s32[2]{0:T(128)S(1)} %pad_add_fusion.me_ref, s32[4]{0:T(128)S(1)} %bitcast.53, bf16[640,1024]{1,0:T(8,128)(2,1)S(1)} %get-tuple-element.324.left_ref, bf16[1024,640]{1,0:T(8,128)(2,1)S(1)} %get-tuple-element.325.back_ref), custom_call_target="tpu_custom_call" | custom-call | flops 36800000000 | tf_op jit(solution)/shard_map/conv_gradient/pallas_call | solution.py:598
  92.4 7.8 %back_through_conv.1 = (bf16[1024,640]{1,0:T(8,128)(2,1)S(1)}, f32[1,640]{1,0:T(1,128)S(1)}, f32[1,640]{1,0:T(1,128)S(1)}, f32[1,640]{1,0:T(1,128)S(1)}) custom-call(bf16[1024,3200]{1,0:T(8,128)(2,1)S(1)} %get-tuple-element.329.taps_ref, bf16[640,3200]{1,0:T(8,128)(2,1)S(1)} %get-tuple-element.330.w_ref, f32[1024,640]{1,0:T(8,128)S(1)} %get-tuple-element.331.n_ref, ...), custom_call_target="tpu_custom_call" | custom-call | flops 46000001024 | tf_op jit(solution)/shard_map/back_through_conv/pallas_call | solution.py:621
  100.1 0.5 add_convert_fusion
  100.9 2.1 %collective-permute-start.18 = (bf16[4,208,128]{2,1,0:T(8,128)(2,1)S(1)}, bf16[4,208,128]{2,1,0:T(8,128)(2,1)S(1)}, u32[]{:S(2)}, u32[]{:S(2)}) collective-permute-start(bf16[4,208,128]{2,1,0:T(8,128)(2,1)S(1)} %get-tuple-element.346), channel_id=1, source_target_pairs={{0,16},{1,17},{2,18},{3,19},{4,20},{5,21},{6,22},{7,23},{8,9},{9,8... | collective-permute-start | bytes 638984 | tf_op jit(solution)/shard_map/ppermute | solution.py:820
  103.0 3.8 %in_gradient.1 = (bf16[16,208,128]{2,1,0:T(8,128)(2,1)S(1)}, bf16[16,208,128]{2,1,0:T(8,128)(2,1)S(1)}) custom-call(s32[2]{0:T(128)S(1)} %pad_add_fusion.me_ref, bf16[1280,1024]{1,0:T(8,128)(2,1)S(1)} %copy-done.20, bf16[1024,640]{1,0:T(8,128)(2,1)S(1)} %get-tuple-element.370.right_ref.back_ref), custom_call_target="tpu_custom_call" | custom-call | flops 17020000256 | tf_op jit(solution)/shard_map/in_gradient/pallas_call | solution.py:530
  106.8 3.8 %block_result.1 = bf16[1024,1280]{1,0:T(8,128)(2,1)} custom-call(bf16[1024,1280]{1,0:T(8,128)(2,1)S(1)} %bitcast.39, bf16[1024,640]{1,0:T(8,128)(2,1)S(1)} %copy-done.22, bf16[640,1280]{1,0:T(8,128)(2,1)S(1)} %get-tuple-element.353.w_ref, f32[1,7680]{1,0:T(1,128)S(1)} %reshape.100.vec_ref), custom_call_target="tpu_custom_call" | custom-call | flops 17479999488 | tf_op jit(solution)/shard_map/block_result/pallas_call | solution.py:575
  110.6 0.3 add_convert_fusion.4
  110.9 2.1 %collective-permute-start.21 = (bf16[8,208,128]{2,1,0:T(8,128)(2,1)S(1)}, bf16[8,208,128]{2,1,0:T(8,128)(2,1)S(1)}, u32[]{:S(2)}, u32[]{:S(2)}) collective-permute-start(bf16[8,208,128]{2,1,0:T(8,128)(2,1)S(1)} %get-tuple-element.361), channel_id=1, source_target_pairs={{0,2},{1,3},{2,0},{3,1},{4,6},{5,7},{6,4},{7,5},{8,12},{9,13},{10,... | collective-permute-start | bytes 1277960 | tf_op jit(solution)/shard_map/ppermute | solution.py:820
  113.0 2.6 %collective-permute-done.19 = bf16[8,512,128]{2,1,0:T(8,128)(2,1)S(1)} collective-permute-done((bf16[8,512,128]{2,1,0:T(8,128)(2,1)S(1)}, bf16[8,512,128]{2,1,0:T(8,128)(2,1)S(1)}, u32[]{:S(2)}, u32[]{:S(2)}) %collective-permute-start.19) | collective-permute-done | bytes 1048608 | tf_op jit(solution)/shard_map/ppermute | solution.py:820
  115.6 0.3 add_convert_fusion.2
  115.9 1.9 %collective-permute-done.18 = bf16[4,208,128]{2,1,0:T(8,128)(2,1)S(1)} collective-permute-done((bf16[4,208,128]{2,1,0:T(8,128)(2,1)S(1)}, bf16[4,208,128]{2,1,0:T(8,128)(2,1)S(1)}, u32[]{:S(2)}, u32[]{:S(2)}) %collective-permute-start.18) | collective-permute-done | bytes 213024 | tf_op jit(solution)/shard_map/ppermute | solution.py:820
  117.9 0.2 collective-permute-start.23
  118.1 8.3 %back_through_in.1 = (bf16[1024,1280]{1,0:T(8,128)(2,1)}, f32[1,1280]{1,0:T(1,128)S(1)}, f32[1,1280]{1,0:T(1,128)S(1)}) custom-call(bf16[1024,640]{1,0:T(8,128)(2,1)S(1)} %get-tuple-element.370.right_ref.back_ref, bf16[1280,640]{1,0:T(8,128)(2,1)S(1)} %get-tuple-element.371.w_ref, bf16[1024,1280]{1,0:T(8,128)(2,1)S(1)} %bitcast.40, ...), custom_call_target="tpu_custom_call" | custom-call | flops 43240001536 | tf_op jit(solution)/shard_map/back_through_in/pallas_call | solution.py:655
  126.5 1.4 collective-permute-start.22
  128.0 1.5 collective-permute-start.27
  129.6 1.3 collective-permute-start.26
  130.9 1.6 collective-permute-done.22
  132.5 2.2 %collective-permute-start.25 = (bf16[2,208,128]{2,1,0:T(8,128)(2,1)S(1)}, bf16[2,208,128]{2,1,0:T(8,128)(2,1)S(1)}, u32[]{:S(2)}, u32[]{:S(2)}) collective-permute-start(bf16[2,208,128]{2,1,0:T(8,128)(2,1)S(1)} %get-tuple-element.393), channel_id=1, source_target_pairs={{0,1},{1,0},{2,3},{3,2},{4,5},{5,4},{6,7},{7,6},{8,24},{9,25},{10,... | collective-permute-start | bytes 319496 | tf_op jit(solution)/shard_map/ppermute | solution.py:820
  134.7 2.2 %collective-permute-done.27 = bf16[2,512,128]{2,1,0:T(8,128)(2,1)S(1)} collective-permute-done((bf16[2,512,128]{2,1,0:T(8,128)(2,1)S(1)}, bf16[2,512,128]{2,1,0:T(8,128)(2,1)S(1)}, u32[]{:S(2)}, u32[]{:S(2)}) %collective-permute-start.27) | collective-permute-done | bytes 262176 | tf_op jit(solution)/shard_map/ppermute | solution.py:820
  136.9 0.4 collective-permute-done.25
  137.4 3.0 %collective-permute-start.28 = (bf16[1,208,128]{2,1,0:T(8,128)(2,1)S(1)}, bf16[1,208,128]{2,1,0:T(8,128)(2,1)S(1)}, u32[]{:S(2)}, u32[]{:S(2)}) collective-permute-start(bf16[1,208,128]{2,1,0:T(8,128)(2,1)S(1)} %get-tuple-element.403), channel_id=1, source_target_pairs={{0,4},{1,5},{2,6},{3,7},{4,0},{5,1},{6,2},{7,3},{8,10},{9,11},{10,... | collective-permute-start | bytes 159752 | tf_op jit(solution)/shard_map/ppermute | solution.py:820
  140.5 2.0 %collective-permute-done.28 = bf16[1,208,128]{2,1,0:T(8,128)(2,1)S(1)} collective-permute-done((bf16[1,208,128]{2,1,0:T(8,128)(2,1)S(1)}, bf16[1,208,128]{2,1,0:T(8,128)(2,1)S(1)}, u32[]{:S(2)}, u32[]{:S(2)}) %collective-permute-start.28) | collective-permute-done | bytes 53280 | tf_op jit(solution)/shard_map/ppermute | solution.py:820
  142.5 4.2 %collective-permute-done.29 = bf16[1,512,128]{2,1,0:T(8,128)(2,1)S(1)} collective-permute-done((bf16[1,512,128]{2,1,0:T(8,128)(2,1)S(1)}, bf16[1,512,128]{2,1,0:T(8,128)(2,1)S(1)}, u32[]{:S(2)}, u32[]{:S(2)}) %collective-permute-start.29) | collective-permute-done | bytes 131104 | tf_op jit(solution)/shard_map/ppermute | solution.py:820
  147.1 1.2 collective-permute-done.30
  148.3 0.2 collective-permute-start.31
  148.4 4.6 %collective-permute-done.31 = f32[64,128]{1,0:T(8,128)S(1)} collective-permute-done((f32[64,128]{1,0:T(8,128)S(1)}, f32[64,128]{1,0:T(8,128)S(1)}, u32[]{:S(2)}, u32[]{:S(2)}) %collective-permute-start.31) | collective-permute-done | bytes 32800 | tf_op jit(solution)/shard_map/ppermute | solution.py:834
  153.1 3.9 %collective-permute-done.32 = f32[64,128]{1,0:T(8,128)S(1)} collective-permute-done((f32[64,128]{1,0:T(8,128)S(1)}, f32[64,128]{1,0:T(8,128)S(1)}, u32[]{:S(2)}, u32[]{:S(2)}) %collective-permute-start.32) | collective-permute-done | bytes 32800 | tf_op jit(solution)/shard_map/ppermute | solution.py:834
  157.0 2.0 %collective-permute-start.33 = (f32[64,128]{1,0:T(8,128)S(1)}, f32[64,128]{1,0:T(8,128)S(1)}, u32[]{:S(2)}, u32[]{:S(2)}) collective-permute-start(f32[64,128]{1,0:T(8,128)S(1)} %add.129), channel_id=1, source_target_pairs={{0,1},{1,0},{2,3},{3,2},{4,5},{5,4},{6,7},{7,6},{8,24},{9,25},{10,... | collective-permute-start | bytes 98312 | tf_op jit(solution)/shard_map/ppermute | solution.py:834
  159.0 2.2 %collective-permute-done.33 = f32[64,128]{1,0:T(8,128)S(1)} collective-permute-done((f32[64,128]{1,0:T(8,128)S(1)}, f32[64,128]{1,0:T(8,128)S(1)}, u32[]{:S(2)}, u32[]{:S(2)}) %collective-permute-start.33) | collective-permute-done | bytes 32800 | tf_op jit(solution)/shard_map/ppermute | solution.py:834
  161.3 0.8 collective-permute-start.34
  162.1 3.1 %collective-permute-done.34 = f32[64,128]{1,0:T(8,128)S(1)} collective-permute-done((f32[64,128]{1,0:T(8,128)S(1)}, f32[64,128]{1,0:T(8,128)S(1)}, u32[]{:S(2)}, u32[]{:S(2)}) %collective-permute-start.34) | collective-permute-done | bytes 32800 | tf_op jit(solution)/shard_map/ppermute | solution.py:834
  165.3 2.1 %update_all.1 = (f32[1,1]{1,0:T(1,128)}, f32[160,160]{1,0:T(8,128)}, f32[160,160]{1,0:T(8,128)}, f32[160,160]{1,0:T(8,128)}, f32[400,160]{1,0:T(8,128)}, /*index...) custom-call(f32[208,128]{1,0:T(8,128)S(1)} %get-tuple-element.451.re, ...), custom_call_target="tpu_custom_call" | custom-call | flops 9200000000 | tf_op jit(solution)/shard_map/update_all/pallas_call | solution.py:746
  (121 shorter events, 3.0 us)
Async XLA Ops:
  0.6 5.1 %copy-start.5 = (f32[5,80,160]{2,1,0:T(8,128)S(1)}, f32[5,80,160]{2,1,0:T(8,128)}, u32[]{:S(2)}) copy-start(f32[5,80,160]{2,1,0:T(8,128)} %param.21) | copy-start | bytes 768004
  0.7 1.0 copy-start.9
  1.7 11.3 %collective-permute-start.1 = (bf16[1,208,128]{2,1,0:T(8,128)(2,1)S(1)}, bf16[1,208,128]{2,1,0:T(8,128)(2,1)}, u32[]{:S(2)}, u32[]{:S(2)}) collective-permute-start(bf16[1,208,128]{2,1,0:T(8,128)(2,1)S(1)} %bitcast.34), channel_id=1, source_target_pairs={{0,4},{1,5},{2,6},{3,7},{4,0},{5,1},{6,2},{7,3},{8,10},{9,11},{10,... | collective-permute-start | bytes 159752 | tf_op jit(solution)/shard_map/ppermute | solution.py:782
  5.8 0.8 copy-start
  5.8 0.9 copy-start.13
  5.9 9.5 %collective-permute-start = (bf16[1,512,128]{2,1,0:T(8,128)(2,1)S(1)}, bf16[1,512,128]{2,1,0:T(8,128)(2,1)S(1)}, u32[]{:S(2)}, u32[]{:S(2)}) collective-permute-start(bf16[1,512,128]{2,1,0:T(8,128)(2,1)S(1)} %bitcast.30), channel_id=1, source_target_pairs={{0,4},{1,5},{2,6},{3,7},{4,0},{5,1},{6,2},{7,3},{8,10},{9,11},{10,... | collective-permute-start | bytes 393224 | tf_op jit(solution)/shard_map/ppermute | solution.py:782
  6.7 0.7 copy-start.25
  6.7 1.8 %copy-start.2 = (bf16[1,1024,1280]{2,1,0:T(8,128)(2,1)S(1)}, bf16[1,1024,1280]{2,1,0:T(8,128)(2,1)}, u32[]{:S(2)}) copy-start(bf16[1,1024,1280]{2,1,0:T(8,128)(2,1)} %param.15) | copy-start | bytes 7864324
  8.5 1.7 %copy-start.3 = (bf16[1,1024,1280]{2,1,0:T(8,128)(2,1)S(1)}, bf16[1,1024,1280]{2,1,0:T(8,128)(2,1)}, u32[]{:S(2)}) copy-start(bf16[1,1024,1280]{2,1,0:T(8,128)(2,1)} %param.16) | copy-start | bytes 7864324
  13.9 8.3 %collective-permute-start.3 = (bf16[2,208,128]{2,1,0:T(8,128)(2,1)S(1)}, bf16[2,208,128]{2,1,0:T(8,128)(2,1)S(1)}, u32[]{:S(2)}, u32[]{:S(2)}) collective-permute-start(bf16[2,208,128]{2,1,0:T(8,128)(2,1)S(1)} %constant_dynamic-update-slice_fusion), channel_id=1, source_target_pairs={{0,1},{1,0},{2,3},{3,2},{4,5},{5,4},{6,7},{7,6},{8,24},{9,25},{10,... | collective-permute-start | bytes 319496 | tf_op jit(solution)/shard_map/ppermute | solution.py:782
  15.5 11.0 %collective-permute-start.6 = (bf16[1,208,128]{2,1,0:T(8,128)(2,1)S(1)}, bf16[1,208,128]{2,1,0:T(8,128)(2,1)S(1)}, u32[]{:S(2)}, u32[]{:S(2)}) collective-permute-start(bf16[1,208,128]{2,1,0:T(8,128)(2,1)S(1)} %bitcast.32), channel_id=1, source_target_pairs={{0,4},{1,5},{2,6},{3,7},{4,0},{5,1},{6,2},{7,3},{8,10},{9,11},{10,... | collective-permute-start | bytes 159752 | tf_op jit(solution)/shard_map/ppermute | solution.py:782
  17.7 8.7 %collective-permute-start.2 = (bf16[2,512,128]{2,1,0:T(8,128)(2,1)S(1)}, bf16[2,512,128]{2,1,0:T(8,128)(2,1)S(1)}, u32[]{:S(2)}, u32[]{:S(2)}) collective-permute-start(bf16[2,512,128]{2,1,0:T(8,128)(2,1)S(1)} %constant_dynamic-update-slice_fusion.2), channel_id=1, source_target_pairs={{0,2},{1,3},{2,0},{3,1},{4,6},{5,7},{6,4},{7,5},{8,12},{9,13},{10,... | collective-permute-start | bytes 786440 | tf_op jit(solution)/shard_map/ppermute | solution.py:782
  22.1 13.7 %copy-start.19 = (bf16[1280,1024]{1,0:T(8,128)(2,1)}, bf16[1280,1024]{1,0:T(8,128)(2,1)S(1)}, u32[]{:S(2)}) copy-start(bf16[1280,1024]{1,0:T(8,128)(2,1)S(1)} %get-tuple-element.348.left_ref) | copy-start | bytes 7864324
  22.1 13.7 %copy-start.23 = (f32[1024,128]{1,0:T(8,128)}, f32[1024,128]{1,0:T(8,128)S(1)}, u32[]{:S(2)}) copy-start(f32[1024,128]{1,0:T(8,128)S(1)} %get-tuple-element.374.stat_ref) | copy-start | bytes 1572868
  22.2 6.7 %collective-permute-start.5 = (bf16[4,208,128]{2,1,0:T(8,128)(2,1)S(1)}, bf16[4,208,128]{2,1,0:T(8,128)(2,1)S(1)}, u32[]{:S(2)}, u32[]{:S(2)}) collective-permute-start(bf16[4,208,128]{2,1,0:T(8,128)(2,1)S(1)} %constant_dynamic-update-slice_fusion.4), channel_id=1, source_target_pairs={{0,16},{1,17},{2,18},{3,19},{4,20},{5,21},{6,22},{7,23},{8,9},{9,8... | collective-permute-start | bytes 638984 | tf_op jit(solution)/shard_map/ppermute | solution.py:782
  26.5 9.2 %collective-permute-start.4 = (bf16[4,512,128]{2,1,0:T(8,128)(2,1)S(1)}, bf16[4,512,128]{2,1,0:T(8,128)(2,1)S(1)}, u32[]{:S(2)}, u32[]{:S(2)}) collective-permute-start(bf16[4,512,128]{2,1,0:T(8,128)(2,1)S(1)} %constant_dynamic-update-slice_fusion.6), channel_id=1, source_target_pairs={{0,1},{1,0},{2,3},{3,2},{4,5},{5,4},{6,7},{7,6},{8,24},{9,25},{10,... | collective-permute-start | bytes 1572872 | tf_op jit(solution)/shard_map/ppermute | solution.py:782
  28.9 12.3 %collective-permute-start.9 = (bf16[8,208,128]{2,1,0:T(8,128)(2,1)S(1)}, bf16[8,208,128]{2,1,0:T(8,128)(2,1)S(1)}, u32[]{:S(2)}, u32[]{:S(2)}) collective-permute-start(bf16[8,208,128]{2,1,0:T(8,128)(2,1)S(1)} %constant_dynamic-update-slice_fusion.10), channel_id=1, source_target_pairs={{0,2},{1,3},{2,0},{3,1},{4,6},{5,7},{6,4},{7,5},{8,12},{9,13},{10,... | collective-permute-start | bytes 1277960 | tf_op jit(solution)/shard_map/ppermute | solution.py:782
  41.3 2.6 %collective-permute-start.10 = (bf16[16,208,128]{2,1,0:T(8,128)(2,1)S(1)}, bf16[16,208,128]{2,1,0:T(8,128)(2,1)S(1)}, u32[]{:S(2)}, u32[]{:S(2)}) collective-permute-start(bf16[16,208,128]{2,1,0:T(8,128)(2,1)S(1)} %constant_dynamic-update-slice_fusion.14.own_ref), channel_id=1, source_target_pairs={{0,8},{1,9},{2,10},{3,11},{4,12},{5,13},{6,14},{7,15},{8,0},{9,1},... | collective-permute-start | bytes 2555912 | tf_op jit(solution)/shard_map/ppermute | solution.py:782
  41.4 15.3 %collective-permute-start.7 = (bf16[8,512,128]{2,1,0:T(8,128)(2,1)S(1)}, bf16[8,512,128]{2,1,0:T(8,128)(2,1)S(1)}, u32[]{:S(2)}, u32[]{:S(2)}) collective-permute-start(bf16[8,512,128]{2,1,0:T(8,128)(2,1)S(1)} %constant_dynamic-update-slice_fusion.12), channel_id=1, source_target_pairs={{0,16},{1,17},{2,18},{3,19},{4,20},{5,21},{6,22},{7,23},{8,9},{9,8... | collective-permute-start | bytes 3145736 | tf_op jit(solution)/shard_map/ppermute | solution.py:782
  43.9 8.6 %collective-permute-start.8 = (bf16[2,208,128]{2,1,0:T(8,128)(2,1)S(1)}, bf16[2,208,128]{2,1,0:T(8,128)(2,1)S(1)}, u32[]{:S(2)}, u32[]{:S(2)}) collective-permute-start(bf16[2,208,128]{2,1,0:T(8,128)(2,1)S(1)} %constant_dynamic-update-slice_fusion.8), channel_id=1, source_target_pairs={{0,2},{1,3},{2,0},{3,1},{4,6},{5,7},{6,4},{7,5},{8,12},{9,13},{10,... | collective-permute-start | bytes 319496 | tf_op jit(solution)/shard_map/ppermute | solution.py:782
  56.9 4.2 %collective-permute-start.11 = (bf16[16,512,128]{2,1,0:T(8,128)(2,1)S(1)}, bf16[16,512,128]{2,1,0:T(8,128)(2,1)S(1)}, u32[]{:S(2)}, u32[]{:S(2)}) collective-permute-start(bf16[16,512,128]{2,1,0:T(8,128)(2,1)S(1)} %constant_dynamic-update-slice_fusion.18.own_ref), channel_id=1, source_target_pairs={{0,8},{1,9},{2,10},{3,11},{4,12},{5,13},{6,14},{7,15},{8,0},{9,1},... | collective-permute-start | bytes 6291464 | tf_op jit(solution)/shard_map/ppermute | solution.py:782
  57.0 5.9 %collective-permute-start.12 = (bf16[4,208,128]{2,1,0:T(8,128)(2,1)S(1)}, bf16[4,208,128]{2,1,0:T(8,128)(2,1)S(1)}, u32[]{:S(2)}, u32[]{:S(2)}) collective-permute-start(bf16[4,208,128]{2,1,0:T(8,128)(2,1)S(1)} %constant_dynamic-update-slice_fusion.16), channel_id=1, source_target_pairs={{0,1},{1,0},{2,3},{3,2},{4,5},{5,4},{6,7},{7,6},{8,24},{9,25},{10,... | collective-permute-start | bytes 638984 | tf_op jit(solution)/shard_map/ppermute | solution.py:782
  63.0 11.1 %copy-start.4 = (bf16[1,1024,1280]{2,1,0:T(8,128)(2,1)S(1)}, bf16[1,1024,1280]{2,1,0:T(8,128)(2,1)}, u32[]{:S(2)}) copy-start(bf16[1,1024,1280]{2,1,0:T(8,128)(2,1)} %param.16) | copy-start | bytes 7864324
  63.0 10.9 %collective-permute-start.13 = (bf16[8,208,128]{2,1,0:T(8,128)(2,1)S(1)}, bf16[8,208,128]{2,1,0:T(8,128)(2,1)S(1)}, u32[]{:S(2)}, u32[]{:S(2)}) collective-permute-start(bf16[8,208,128]{2,1,0:T(8,128)(2,1)S(1)} %constant_dynamic-update-slice_fusion.20), channel_id=1, source_target_pairs={{0,16},{1,17},{2,18},{3,19},{4,20},{5,21},{6,22},{7,23},{8,9},{9,8... | collective-permute-start | bytes 1277960 | tf_op jit(solution)/shard_map/ppermute | solution.py:782
  73.8 3.2 %copy-start.21 = (bf16[1024,640]{1,0:T(8,128)(2,1)}, bf16[1024,640]{1,0:T(8,128)(2,1)S(1)}, u32[]{:S(2)}) copy-start(bf16[1024,640]{1,0:T(8,128)(2,1)S(1)} %get-tuple-element.352.h_ref) | copy-start | bytes 3932164
  74.0 3.7 %collective-permute-start.14 = (bf16[16,208,128]{2,1,0:T(8,128)(2,1)S(1)}, bf16[16,208,128]{2,1,0:T(8,128)(2,1)S(1)}, u32[]{:S(2)}, u32[]{:S(2)}) collective-permute-start(bf16[16,208,128]{2,1,0:T(8,128)(2,1)S(1)} %constant_dynamic-update-slice_fusion.22.own_ref), channel_id=1, source_target_pairs={{0,8},{1,9},{2,10},{3,11},{4,12},{5,13},{6,14},{7,15},{8,0},{9,1},... | collective-permute-start | bytes 2555912 | tf_op jit(solution)/shard_map/ppermute | solution.py:782
  77.1 6.6 %collective-permute-start.15 = (bf16[16,208,128]{2,1,0:T(8,128)(2,1)S(1)}, bf16[16,208,128]{2,1,0:T(8,128)(2,1)S(1)}, u32[]{:S(2)}, u32[]{:S(2)}) collective-permute-start(bf16[16,208,128]{2,1,0:T(8,128)(2,1)S(1)} %get-tuple-element.317), channel_id=1, source_target_pairs={{0,8},{1,9},{2,10},{3,11},{4,12},{5,13},{6,14},{7,15},{8,0},{9,1},... | collective-permute-start | bytes 2555912 | tf_op jit(solution)/shard_map/ppermute | solution.py:810
  83.9 16.8 %collective-permute-start.16 = (bf16[8,208,128]{2,1,0:T(8,128)(2,1)S(1)}, bf16[8,208,128]{2,1,0:T(8,128)(2,1)S(1)}, u32[]{:S(2)}, u32[]{:S(2)}) collective-permute-start(bf16[8,208,128]{2,1,0:T(8,128)(2,1)S(1)} %get-tuple-element.321), channel_id=1, source_target_pairs={{0,2},{1,3},{2,0},{3,1},{4,6},{5,7},{6,4},{7,5},{8,12},{9,13},{10,... | collective-permute-start | bytes 1277960 | tf_op jit(solution)/shard_map/ppermute | solution.py:820
  92.3 7.9 %collective-permute-start.17 = (bf16[16,512,128]{2,1,0:T(8,128)(2,1)S(1)}, bf16[16,512,128]{2,1,0:T(8,128)(2,1)S(1)}, u32[]{:S(2)}, u32[]{:S(2)}) collective-permute-start(bf16[16,512,128]{2,1,0:T(8,128)(2,1)S(1)} %get-tuple-element.337), channel_id=1, source_target_pairs={{0,8},{1,9},{2,10},{3,11},{4,12},{5,13},{6,14},{7,15},{8,0},{9,1},... | collective-permute-start | bytes 6291464 | tf_op jit(solution)/shard_map/ppermute | solution.py:810
  100.1 2.9 %copy-start.20 = (bf16[1280,1024]{1,0:T(8,128)(2,1)S(1)}, bf16[1280,1024]{1,0:T(8,128)(2,1)}, u32[]{:S(2)}) copy-start(bf16[1280,1024]{1,0:T(8,128)(2,1)} %copy-done.19) | copy-start | bytes 7864324
  100.7 14.9 %collective-permute-start.19 = (bf16[8,512,128]{2,1,0:T(8,128)(2,1)S(1)}, bf16[8,512,128]{2,1,0:T(8,128)(2,1)S(1)}, u32[]{:S(2)}, u32[]{:S(2)}) collective-permute-start(bf16[8,512,128]{2,1,0:T(8,128)(2,1)S(1)} %get-tuple-element.342), channel_id=1, source_target_pairs={{0,16},{1,17},{2,18},{3,19},{4,20},{5,21},{6,22},{7,23},{8,9},{9,8... | collective-permute-start | bytes 3145736 | tf_op jit(solution)/shard_map/ppermute | solution.py:820
  100.9 16.9 %collective-permute-start.18 = (bf16[4,208,128]{2,1,0:T(8,128)(2,1)S(1)}, bf16[4,208,128]{2,1,0:T(8,128)(2,1)S(1)}, u32[]{:S(2)}, u32[]{:S(2)}) collective-permute-start(bf16[4,208,128]{2,1,0:T(8,128)(2,1)S(1)} %get-tuple-element.346), channel_id=1, source_target_pairs={{0,16},{1,17},{2,18},{3,19},{4,20},{5,21},{6,22},{7,23},{8,9},{9,8... | collective-permute-start | bytes 638984 | tf_op jit(solution)/shard_map/ppermute | solution.py:820
  103.0 3.8 %copy-start.22 = (bf16[1024,640]{1,0:T(8,128)(2,1)S(1)}, bf16[1024,640]{1,0:T(8,128)(2,1)}, u32[]{:S(2)}) copy-start(bf16[1024,640]{1,0:T(8,128)(2,1)} %copy-done.21) | copy-start | bytes 3932164
  106.7 3.9 %collective-permute-start.20 = (bf16[16,208,128]{2,1,0:T(8,128)(2,1)S(1)}, bf16[16,208,128]{2,1,0:T(8,128)(2,1)S(1)}, u32[]{:S(2)}, u32[]{:S(2)}) collective-permute-start(bf16[16,208,128]{2,1,0:T(8,128)(2,1)S(1)} %get-tuple-element.357), channel_id=1, source_target_pairs={{0,8},{1,9},{2,10},{3,11},{4,12},{5,13},{6,14},{7,15},{8,0},{9,1},... | collective-permute-start | bytes 2555912 | tf_op jit(solution)/shard_map/ppermute | solution.py:810
  110.9 7.2 %copy-start.24 = (f32[1024,128]{1,0:T(8,128)S(1)}, f32[1024,128]{1,0:T(8,128)}, u32[]{:S(2)}) copy-start(f32[1024,128]{1,0:T(8,128)} %copy-done.23) | copy-start | bytes 1572868
  110.9 15.5 %collective-permute-start.21 = (bf16[8,208,128]{2,1,0:T(8,128)(2,1)S(1)}, bf16[8,208,128]{2,1,0:T(8,128)(2,1)S(1)}, u32[]{:S(2)}, u32[]{:S(2)}) collective-permute-start(bf16[8,208,128]{2,1,0:T(8,128)(2,1)S(1)} %get-tuple-element.361), channel_id=1, source_target_pairs={{0,2},{1,3},{2,0},{3,1},{4,6},{5,7},{6,4},{7,5},{8,12},{9,13},{10,... | collective-permute-start | bytes 1277960 | tf_op jit(solution)/shard_map/ppermute | solution.py:820
  115.8 12.0 %collective-permute-start.24 = (bf16[4,512,128]{2,1,0:T(8,128)(2,1)S(1)}, bf16[4,512,128]{2,1,0:T(8,128)(2,1)S(1)}, u32[]{:S(2)}, u32[]{:S(2)}) collective-permute-start(bf16[4,512,128]{2,1,0:T(8,128)(2,1)S(1)} %get-tuple-element.365), channel_id=1, source_target_pairs={{0,1},{1,0},{2,3},{3,2},{4,5},{5,4},{6,7},{7,6},{8,24},{9,25},{10,... | collective-permute-start | bytes 1572872 | tf_op jit(solution)/shard_map/ppermute | solution.py:820
  117.9 11.6 %collective-permute-start.23 = (bf16[2,208,128]{2,1,0:T(8,128)(2,1)S(1)}, bf16[2,208,128]{2,1,0:T(8,128)(2,1)S(1)}, u32[]{:S(2)}, u32[]{:S(2)}) collective-permute-start(bf16[2,208,128]{2,1,0:T(8,128)(2,1)S(1)} %get-tuple-element.369), channel_id=1, source_target_pairs={{0,1},{1,0},{2,3},{3,2},{4,5},{5,4},{6,7},{7,6},{8,24},{9,25},{10,... | collective-permute-start | bytes 319496 | tf_op jit(solution)/shard_map/ppermute | solution.py:820
  126.5 5.9 %collective-permute-start.22 = (bf16[4,208,128]{2,1,0:T(8,128)(2,1)S(1)}, bf16[4,208,128]{2,1,0:T(8,128)(2,1)S(1)}, u32[]{:S(2)}, u32[]{:S(2)}) collective-permute-start(bf16[4,208,128]{2,1,0:T(8,128)(2,1)S(1)} %get-tuple-element.381), channel_id=1, source_target_pairs={{0,16},{1,17},{2,18},{3,19},{4,20},{5,21},{6,22},{7,23},{8,9},{9,8... | collective-permute-start | bytes 638984 | tf_op jit(solution)/shard_map/ppermute | solution.py:820
  128.0 8.9 %collective-permute-start.27 = (bf16[2,512,128]{2,1,0:T(8,128)(2,1)S(1)}, bf16[2,512,128]{2,1,0:T(8,128)(2,1)S(1)}, u32[]{:S(2)}, u32[]{:S(2)}) collective-permute-start(bf16[2,512,128]{2,1,0:T(8,128)(2,1)S(1)} %get-tuple-element.385), channel_id=1, source_target_pairs={{0,2},{1,3},{2,0},{3,1},{4,6},{5,7},{6,4},{7,5},{8,12},{9,13},{10,... | collective-permute-start | bytes 786440 | tf_op jit(solution)/shard_map/ppermute | solution.py:820
  129.6 7.4 %collective-permute-start.26 = (bf16[1,208,128]{2,1,0:T(8,128)(2,1)S(1)}, bf16[1,208,128]{2,1,0:T(8,128)(2,1)S(1)}, u32[]{:S(2)}, u32[]{:S(2)}) collective-permute-start(bf16[1,208,128]{2,1,0:T(8,128)(2,1)S(1)} %get-tuple-element.389), channel_id=1, source_target_pairs={{0,4},{1,5},{2,6},{3,7},{4,0},{5,1},{6,2},{7,3},{8,10},{9,11},{10,... | collective-permute-start | bytes 159752 | tf_op jit(solution)/shard_map/ppermute | solution.py:820
  132.5 4.9 %collective-permute-start.25 = (bf16[2,208,128]{2,1,0:T(8,128)(2,1)S(1)}, bf16[2,208,128]{2,1,0:T(8,128)(2,1)S(1)}, u32[]{:S(2)}, u32[]{:S(2)}) collective-permute-start(bf16[2,208,128]{2,1,0:T(8,128)(2,1)S(1)} %get-tuple-element.393), channel_id=1, source_target_pairs={{0,1},{1,0},{2,3},{3,2},{4,5},{5,4},{6,7},{7,6},{8,24},{9,25},{10,... | collective-permute-start | bytes 319496 | tf_op jit(solution)/shard_map/ppermute | solution.py:820
  137.4 5.1 %collective-permute-start.28 = (bf16[1,208,128]{2,1,0:T(8,128)(2,1)S(1)}, bf16[1,208,128]{2,1,0:T(8,128)(2,1)S(1)}, u32[]{:S(2)}, u32[]{:S(2)}) collective-permute-start(bf16[1,208,128]{2,1,0:T(8,128)(2,1)S(1)} %get-tuple-element.403), channel_id=1, source_target_pairs={{0,4},{1,5},{2,6},{3,7},{4,0},{5,1},{6,2},{7,3},{8,10},{9,11},{10,... | collective-permute-start | bytes 159752 | tf_op jit(solution)/shard_map/ppermute | solution.py:820
  140.4 6.4 %collective-permute-start.29 = (bf16[1,512,128]{2,1,0:T(8,128)(2,1)S(1)}, bf16[1,512,128]{2,1,0:T(8,128)(2,1)S(1)}, u32[]{:S(2)}, u32[]{:S(2)}) collective-permute-start(bf16[1,512,128]{2,1,0:T(8,128)(2,1)S(1)} %get-tuple-element.397), channel_id=1, source_target_pairs={{0,4},{1,5},{2,6},{3,7},{4,0},{5,1},{6,2},{7,3},{8,10},{9,11},{10,... | collective-permute-start | bytes 393224 | tf_op jit(solution)/shard_map/ppermute | solution.py:820
  146.8 18.4 %copy-start.1 = (f32[7680]{0:T(1024)S(1)}, f32[7680]{0:T(1024)}, u32[]{:S(2)}) copy-start(f32[7680]{0:T(1024)} %param.27) | copy-start | bytes 92164
  146.8 18.4 %copy-start.6 = (f32[5,80,160]{2,1,0:T(8,128)S(1)}, f32[5,80,160]{2,1,0:T(8,128)}, u32[]{:S(2)}) copy-start(f32[5,80,160]{2,1,0:T(8,128)} %param.21) | copy-start | bytes 768004
  146.8 18.4 %copy-start.7 = (f32[5,80,160]{2,1,0:T(8,128)S(1)}, f32[5,80,160]{2,1,0:T(8,128)}, u32[]{:S(2)}) copy-start(f32[5,80,160]{2,1,0:T(8,128)} %param.22) | copy-start | bytes 768004
  146.8 18.4 %copy-start.8 = (f32[5,80,160]{2,1,0:T(8,128)S(1)}, f32[5,80,160]{2,1,0:T(8,128)}, u32[]{:S(2)}) copy-start(f32[5,80,160]{2,1,0:T(8,128)} %param.23) | copy-start | bytes 768004
  146.8 18.4 %copy-start.10 = (f32[160,160]{1,0:T(8,128)S(1)}, f32[160,160]{1,0:T(8,128)}, u32[]{:S(2)}) copy-start(f32[160,160]{1,0:T(8,128)} %refs_4_.1) | copy-start | bytes 307204
  146.8 18.4 %copy-start.11 = (f32[160,160]{1,0:T(8,128)S(1)}, f32[160,160]{1,0:T(8,128)}, u32[]{:S(2)}) copy-start(f32[160,160]{1,0:T(8,128)} %refs_5_.1) | copy-start | bytes 307204
  146.8 18.4 %copy-start.12 = (f32[160,160]{1,0:T(8,128)S(1)}, f32[160,160]{1,0:T(8,128)}, u32[]{:S(2)}) copy-start(f32[160,160]{1,0:T(8,128)} %refs_6_.1) | copy-start | bytes 307204
  146.8 18.4 %copy-start.14 = (f32[80,320]{1,0:T(8,128)S(1)}, f32[80,320]{1,0:T(8,128)}, u32[]{:S(2)}) copy-start(f32[80,320]{1,0:T(8,128)} %refs_10_.1) | copy-start | bytes 307204
  146.9 18.4 %copy-start.15 = (f32[80,320]{1,0:T(8,128)S(1)}, f32[80,320]{1,0:T(8,128)}, u32[]{:S(2)}) copy-start(f32[80,320]{1,0:T(8,128)} %refs_11_.1) | copy-start | bytes 307204
  146.9 18.4 %copy-start.16 = (f32[80,320]{1,0:T(8,128)S(1)}, f32[80,320]{1,0:T(8,128)}, u32[]{:S(2)}) copy-start(f32[80,320]{1,0:T(8,128)} %refs_12_.1) | copy-start | bytes 307204
  146.9 18.4 %copy-start.17 = (f32[7680]{0:T(1024)S(1)}, f32[7680]{0:T(1024)}, u32[]{:S(2)}) copy-start(f32[7680]{0:T(1024)} %param.28) | copy-start | bytes 92164
  146.9 18.4 %copy-start.18 = (f32[7680]{0:T(1024)S(1)}, f32[7680]{0:T(1024)}, u32[]{:S(2)}) copy-start(f32[7680]{0:T(1024)} %param.29) | copy-start | bytes 92164
  147.0 1.3 collective-permute-start.30
  148.3 4.8 %collective-permute-start.31 = (f32[64,128]{1,0:T(8,128)S(1)}, f32[64,128]{1,0:T(8,128)S(1)}, u32[]{:S(2)}, u32[]{:S(2)}) collective-permute-start(f32[64,128]{1,0:T(8,128)S(1)} %add.127), channel_id=1, source_target_pairs={{0,4},{1,5},{2,6},{3,7},{4,0},{5,1},{6,2},{7,3},{8,10},{9,11},{10,... | collective-permute-start | bytes 98312 | tf_op jit(solution)/shard_map/ppermute | solution.py:834
  153.1 3.9 %collective-permute-start.32 = (f32[64,128]{1,0:T(8,128)S(1)}, f32[64,128]{1,0:T(8,128)S(1)}, u32[]{:S(2)}, u32[]{:S(2)}) collective-permute-start(f32[64,128]{1,0:T(8,128)S(1)} %add.128), channel_id=1, source_target_pairs={{0,2},{1,3},{2,0},{3,1},{4,6},{5,7},{6,4},{7,5},{8,12},{9,13},{10,... | collective-permute-start | bytes 98312 | tf_op jit(solution)/shard_map/ppermute | solution.py:834
  157.0 4.2 %collective-permute-start.33 = (f32[64,128]{1,0:T(8,128)S(1)}, f32[64,128]{1,0:T(8,128)S(1)}, u32[]{:S(2)}, u32[]{:S(2)}) collective-permute-start(f32[64,128]{1,0:T(8,128)S(1)} %add.129), channel_id=1, source_target_pairs={{0,1},{1,0},{2,3},{3,2},{4,5},{5,4},{6,7},{7,6},{8,24},{9,25},{10,... | collective-permute-start | bytes 98312 | tf_op jit(solution)/shard_map/ppermute | solution.py:834
  161.3 3.9 %collective-permute-start.34 = (f32[64,128]{1,0:T(8,128)S(1)}, f32[64,128]{1,0:T(8,128)S(1)}, u32[]{:S(2)}, u32[]{:S(2)}) collective-permute-start(f32[64,128]{1,0:T(8,128)S(1)} %add.130), channel_id=1, source_target_pairs={{0,16},{1,17},{2,18},{3,19},{4,20},{5,21},{6,22},{7,23},{8,9},{9,8... | collective-permute-start | bytes 98312 | tf_op jit(solution)/shard_map/ppermute | solution.py:834
where the time goes:
time: 168 us; the launch traced here: 167 us
  Pallas kernels  66.3 us (39%)
  waiting for transfers between devices  55.9 us (33%)
  starting transfers between devices  35 us (21%)
  local copies, waits for them, and re-layouts  6.52 us (4%)
  other arithmetic  2.28 us (1%)
    ppermute x15, waiting for transfers between devices, send(): lax.ppermute(held, AXES, self.net.core() if last else self.net.stage(self...  26 us
    ppermute x15, starting transfers between devices, send(): lax.ppermute(held, AXES, self.net.core() if last else self.net.stage(self...  17.2 us
    ppermute x12, waiting for transfers between devices, step(): self.coming = lax.ppermute(away, AXES, self.net.stage(self.stage))  14.9 us
    ppermute x12, starting transfers between devices, step(): self.coming = lax.ppermute(away, AXES, self.net.stage(self.stage))  13.9 us
    ppermute x4, waiting for transfers between devices, total_sum(): value = value + lax.ppermute(value, AXES, net.stage(stage))  13.8 us
    pallas_call x1, Pallas kernels, mix_two(): call(kernel, 'mix_two', outs, [SMEM, SMEM, ANY, ANY, whole((LENGTH, INNER...  8.75 us
    pallas_call x1, Pallas kernels, mix_one(): call(kernel, 'mix_one', outs, [SMEM, ANY, ANY, whole((LENGTH, D)), whole(...  8.54 us
    pallas_call x1, Pallas kernels, back_through_in(): call(kernel, 'back_through_in', [shape((LENGTH, D), BF16), row, row], [ro...  8.31 us
  transfers between devices with their start and end apart: 35, of which 19 were waited for; matrix products, arithmetic and copies ran while one was open for 2% of the time, Pallas kernels for 38%

commit v1 on v0

--- a/solution.py
+++ b/solution.py
@@ -933,7 +933,6 @@
     block_output = seq.run(block_result, x, h3, full_out, vec)
     sum_in.step()
     sum_conv.step()
-    sum_out.step()
     input_grad, grad_g1, grad_s1 = seq.run(
         back_through_in, back_one, full_in, x, cot, stat, vec
     )
@@ -942,8 +941,9 @@
     sum_out.step()
     sum_in.step()
     sum_conv.step()
+    sum_out.step()
+    sum_in.step()
     grad_out = sum_out.end()
-    sum_in.step()
     grad_conv = sum_conv.end()
     grad_in = sum_in.end()
 

time: 168 us -> 164 us (0.976)
  waiting for transfers between devices: 55.9 us -> 50.4 us
  starting transfers between devices: 35 us -> 37.3 us
    ppermute x12, waiting for transfers between devices: 14.9 us -> 9.51 us  [step(): self.coming = lax.ppermute(away, AXES, self.net.stage(self.stage))]
    ppermute x12, starting transfers between devices: 13.9 us -> 16.3 us  [step(): self.coming = lax.ppermute(away, AXES, self.net.stage(self.stage))]
  transfers between devices with their start and end apart: 35 -> 35, of which waited for: 19 -> 16; matrix products, arithmetic and copies ran while one was open for 2% -> 2% of each run, Pallas kernels for 38% -> 39%
where the time goes in v1:
time: 164 us
  Pallas kernels  66 us (40%)
  waiting for transfers between devices  50.4 us (31%)
  starting transfers between devices  37.3 us (23%)
  local copies, waits for them, and re-layouts  6.52 us (4%)
  other arithmetic  2.25 us (1%)
    ppermute x15, waiting for transfers between devices, send(): lax.ppermute(held, AXES, self.net.core() if last else self.net.stage(self...  26 us
    ppermute x15, starting transfers between devices, send(): lax.ppermute(held, AXES, self.net.core() if last else self.net.stage(self...  17.2 us
    ppermute x12, starting transfers between devices, step(): self.coming = lax.ppermute(away, AXES, self.net.stage(self.stage))  16.3 us
    ppermute x4, waiting for transfers between devices, total_sum(): value = value + lax.ppermute(value, AXES, net.stage(stage))  13.7 us
    ppermute x12, waiting for transfers between devices, step(): self.coming = lax.ppermute(away, AXES, self.net.stage(self.stage))  9.51 us
    pallas_call x1, Pallas kernels, mix_two(): call(kernel, 'mix_two', outs, [SMEM, SMEM, ANY, ANY, whole((LENGTH, INNER...  8.75 us
    pallas_call x1, Pallas kernels, mix_one(): call(kernel, 'mix_one', outs, [SMEM, ANY, ANY, whole((LENGTH, D)), whole(...  8.53 us
    pallas_call x1, Pallas kernels, back_through_in(): call(kernel, 'back_through_in', [shape((LENGTH, D), BF16), row, row], [ro...  8.23 us
  transfers between devices with their start and end apart: 35, of which 16 were waited for; matrix products, arithmetic and copies ran while one was open for 2% of the time, Pallas kernels for 39%

profile of v1, /device:TPU:0, one launch (start us, length us, event | category | flops | bytes accessed | tf_op | source)
XLA Modules:
  0.0 163.9 jit_solution(6635751688852631172)
XLA Ops:
  0.7 1.0 copy-done.9
  1.7 4.1 %collective-permute-start.1 = (bf16[1,208,128]{2,1,0:T(8,128)(2,1)S(1)}, bf16[1,208,128]{2,1,0:T(8,128)(2,1)}, u32[]{:S(2)}, u32[]{:S(2)}) collective-permute-start(bf16[1,208,128]{2,1,0:T(8,128)(2,1)S(1)} %bitcast.34), channel_id=1, source_target_pairs={{0,4},{1,5},{2,6},{3,7},{4,0},{5,1},{6,2},{7,3},{8,10},{9,11},{10,... | collective-permute-start | bytes 159752 | tf_op jit(solution)/shard_map/ppermute | solution.py:782
  6.0 0.6 copy-done
  6.6 0.1 copy-done.13
  6.9 0.5 copy-done.25
  7.4 0.2 reduce-window.9
  7.5 0.9 copy-done.2
  8.5 1.7 %copy-done.3 = bf16[1,1024,1280]{2,1,0:T(8,128)(2,1)S(1)} copy-done((bf16[1,1024,1280]{2,1,0:T(8,128)(2,1)S(1)}, bf16[1,1024,1280]{2,1,0:T(8,128)(2,1)}, u32[]{:S(2)}) %copy-start.3) | copy-done | bytes 2621464
  10.2 2.8 %first_norm.2 = (bf16[1024,1280]{1,0:T(8,128)(2,1)S(1)}, bf16[1280,1024]{1,0:T(8,128)(2,1)S(1)}, f32[1024,128]{1,0:T(8,128)S(1)}, f32[1,1280]{1,0:T(1,128)S(1)}) custom-call(bf16[1024,1280]{1,0:T(8,128)(2,1)S(1)} %bitcast.37, bf16[1024,1280]{1,0:T(8,128)(2,1)S(1)} %bitcast.41, f32[1,7680]{1,0:T(1,128)S(1)} %reshape.100.vec_ref), custom_call_target="tpu_custom_call" | custom-call | flops 12880000000 | tf_op jit(solution)/shard_map/first_norm/pallas_call | solution.py:403
  13.0 0.8 constant_dynamic-update-slice_fusion
  13.9 1.6 collective-permute-start.3
  15.5 2.3 %collective-permute-start.6 = (bf16[1,208,128]{2,1,0:T(8,128)(2,1)S(1)}, bf16[1,208,128]{2,1,0:T(8,128)(2,1)S(1)}, u32[]{:S(2)}, u32[]{:S(2)}) collective-permute-start(bf16[1,208,128]{2,1,0:T(8,128)(2,1)S(1)} %bitcast.32), channel_id=1, source_target_pairs={{0,4},{1,5},{2,6},{3,7},{4,0},{5,1},{6,2},{7,3},{8,10},{9,11},{10,... | collective-permute-start | bytes 159752 | tf_op jit(solution)/shard_map/ppermute | solution.py:782
  17.7 1.6 collective-permute-start.2
  19.3 2.8 %first_norm.3 = (bf16[1024,1280]{1,0:T(8,128)(2,1)S(1)}, bf16[1280,1024]{1,0:T(8,128)(2,1)S(1)}, f32[1024,128]{1,0:T(8,128)S(1)}, f32[1,1280]{1,0:T(1,128)S(1)}) custom-call(bf16[1024,1280]{1,0:T(8,128)(2,1)S(1)} %bitcast.38, bf16[1024,1280]{1,0:T(8,128)(2,1)S(1)} %bitcast.42, ...), custom_call_target="tpu_custom_call", output_to_operand_aliasing={{0}: (3, {}), {1}: (4, {}), {2}: (5, {})} | custom-call | flops 12880000000 | tf_op jit(solution)/shard_map/first_norm/pallas_call | solution.py:403
  22.2 1.6 collective-permute-start.5
  23.8 2.6 %collective-permute-done.2 = bf16[2,512,128]{2,1,0:T(8,128)(2,1)S(1)} collective-permute-done((bf16[2,512,128]{2,1,0:T(8,128)(2,1)S(1)}, bf16[2,512,128]{2,1,0:T(8,128)(2,1)S(1)}, u32[]{:S(2)}, u32[]{:S(2)}) %collective-permute-start.2) | collective-permute-done | bytes 262176 | tf_op jit(solution)/shard_map/ppermute | solution.py:782
  26.5 0.6 collective-permute-start.4
  27.1 1.7 %collective-permute-done.5 = bf16[4,208,128]{2,1,0:T(8,128)(2,1)S(1)} collective-permute-done((bf16[4,208,128]{2,1,0:T(8,128)(2,1)S(1)}, bf16[4,208,128]{2,1,0:T(8,128)(2,1)S(1)}, u32[]{:S(2)}, u32[]{:S(2)}) %collective-permute-start.5) | collective-permute-done | bytes 213024 | tf_op jit(solution)/shard_map/ppermute | solution.py:782
  28.9 0.5 collective-permute-start.9
  29.4 6.3 %collective-permute-done.4 = bf16[4,512,128]{2,1,0:T(8,128)(2,1)S(1)} collective-permute-done((bf16[4,512,128]{2,1,0:T(8,128)(2,1)S(1)}, bf16[4,512,128]{2,1,0:T(8,128)(2,1)S(1)}, u32[]{:S(2)}, u32[]{:S(2)}) %collective-permute-start.4) | collective-permute-done | bytes 524320 | tf_op jit(solution)/shard_map/ppermute | solution.py:782
  35.9 5.3 %collective-permute-done.9 = bf16[8,208,128]{2,1,0:T(8,128)(2,1)S(1)} collective-permute-done((bf16[8,208,128]{2,1,0:T(8,128)(2,1)S(1)}, bf16[8,208,128]{2,1,0:T(8,128)(2,1)S(1)}, u32[]{:S(2)}, u32[]{:S(2)}) %collective-permute-start.9) | collective-permute-done | bytes 426016 | tf_op jit(solution)/shard_map/ppermute | solution.py:782
  41.4 2.5 %collective-permute-start.7 = (bf16[8,512,128]{2,1,0:T(8,128)(2,1)S(1)}, bf16[8,512,128]{2,1,0:T(8,128)(2,1)S(1)}, u32[]{:S(2)}, u32[]{:S(2)}) collective-permute-start(bf16[8,512,128]{2,1,0:T(8,128)(2,1)S(1)} %constant_dynamic-update-slice_fusion.12), channel_id=1, source_target_pairs={{0,16},{1,17},{2,18},{3,19},{4,20},{5,21},{6,22},{7,23},{8,9},{9,8... | collective-permute-start | bytes 3145736 | tf_op jit(solution)/shard_map/ppermute | solution.py:782
  43.9 8.5 %mix_one.1 = (bf16[1024,640]{1,0:T(8,128)(2,1)S(1)}, bf16[640,1024]{1,0:T(8,128)(2,1)S(1)}, f32[1024,640]{1,0:T(8,128)S(1)}, f32[1024,128]{1,0:T(8,128)S(1)}, bf16[1280,640]{1,0:T(8,128)(2,1)S(1)}) custom-call(s32[2]{0:T(128)S(1)} %pad_add_fusion.me_ref, bf16[16,208,128]{2,1,0:T(8,128)(2,1)S(1)} %constant_dynamic-update-slice_fusion.14.own_ref, ...), custom_call_target="tpu_custom_call" | custom-call | flops 46000000 | tf_op jit(solution)/shard_map/mix_one/pallas_call | solution.py:458
  52.5 4.2 %collective-permute-done.7 = bf16[8,512,128]{2,1,0:T(8,128)(2,1)S(1)} collective-permute-done((bf16[8,512,128]{2,1,0:T(8,128)(2,1)S(1)}, bf16[8,512,128]{2,1,0:T(8,128)(2,1)S(1)}, u32[]{:S(2)}, u32[]{:S(2)}) %collective-permute-start.7) | collective-permute-done | bytes 1048608 | tf_op jit(solution)/shard_map/ppermute | solution.py:782
  56.8 0.1 constant_dynamic-update-slice_fusion.18.own_ref
  57.1 4.1 %collective-permute-done.11.peer_ref = bf16[16,512,128]{2,1,0:T(8,128)(2,1)S(1)} collective-permute-done((bf16[16,512,128]{2,1,0:T(8,128)(2,1)S(1)}, bf16[16,512,128]{2,1,0:T(8,128)(2,1)S(1)}, u32[]{:S(2)}, u32[]{:S(2)}) %collective-permute-start.11) | collective-permute-done | bytes 2097184 | tf_op jit(solution)/shard_map/ppermute | solution.py:782
  61.2 1.8 %collective-permute-done.12 = bf16[4,208,128]{2,1,0:T(8,128)(2,1)S(1)} collective-permute-done((bf16[4,208,128]{2,1,0:T(8,128)(2,1)S(1)}, bf16[4,208,128]{2,1,0:T(8,128)(2,1)S(1)}, u32[]{:S(2)}, u32[]{:S(2)}) %collective-permute-start.12) | collective-permute-done | bytes 213024 | tf_op jit(solution)/shard_map/ppermute | solution.py:782
  63.0 2.1 %collective-permute-start.13 = (bf16[8,208,128]{2,1,0:T(8,128)(2,1)S(1)}, bf16[8,208,128]{2,1,0:T(8,128)(2,1)S(1)}, u32[]{:S(2)}, u32[]{:S(2)}) collective-permute-start(bf16[8,208,128]{2,1,0:T(8,128)(2,1)S(1)} %constant_dynamic-update-slice_fusion.20), channel_id=1, source_target_pairs={{0,16},{1,17},{2,18},{3,19},{4,20},{5,21},{6,22},{7,23},{8,9},{9,8... | collective-permute-start | bytes 1277960 | tf_op jit(solution)/shard_map/ppermute | solution.py:782
  65.1 8.8 %mix_two.1 = (bf16[1024,640]{1,0:T(8,128)(2,1)S(1)}, bf16[640,1024]{1,0:T(8,128)(2,1)S(1)}, f32[1024,640]{1,0:T(8,128)S(1)}, f32[1024,128]{1,0:T(8,128)S(1)}, bf16[640,3200]{1,0:T(8,128)(2,1)S(1)}) custom-call(s32[2]{0:T(128)S(1)} %pad_add_fusion.me_ref, s32[4]{0:T(128)S(1)} %bitcast.52, ...), custom_call_target="tpu_custom_call" | custom-call | flops 53819998208 | tf_op jit(solution)/shard_map/mix_two/pallas_call | solution.py:484
  74.0 3.0 %out_gradient.1 = (bf16[16,208,128]{2,1,0:T(8,128)(2,1)S(1)}, bf16[16,208,128]{2,1,0:T(8,128)(2,1)S(1)}) custom-call(s32[2]{0:T(128)S(1)} %pad_add_fusion.me_ref, bf16[640,1024]{1,0:T(8,128)(2,1)S(1)} %get-tuple-element.298.left_ref, bf16[1024,1280]{1,0:T(8,128)(2,1)S(1)} %bitcast.43), custom_call_target="tpu_custom_call" | custom-call | flops 13799999488 | tf_op jit(solution)/shard_map/out_gradient/pallas_call | solution.py:530
  77.1 0.6 collective-permute-start.15
  77.6 6.1 %back_through_out.1 = (bf16[1024,640]{1,0:T(8,128)(2,1)S(1)}, f32[1,640]{1,0:T(1,128)S(1)}, f32[1,640]{1,0:T(1,128)S(1)}, f32[1,640]{1,0:T(1,128)S(1)}, bf16[640,1280]{1,0:T(8,128)(2,1)S(1)}) custom-call(s32[2]{0:T(128)S(1)} %pad_add_fusion.me_ref, bf16[16,208,128]{2,1,0:T(8,128)(2,1)S(1)} %constant_dynamic-update-slice_fusion.22.own_ref, ...), custom_call_target="tpu_custom_call" | custom-call | flops 29440000000 | tf_op jit(solution)/shard_map/back_through_out/pallas_call | solution.py:554
  83.7 0.2 add_convert_fusion.6
  84.0 8.2 %conv_gradient.1 = (bf16[16,512,128]{2,1,0:T(8,128)(2,1)S(1)}, bf16[16,512,128]{2,1,0:T(8,128)(2,1)S(1)}, bf16[1024,3200]{1,0:T(8,128)(2,1)S(1)}) custom-call(s32[2]{0:T(128)S(1)} %pad_add_fusion.me_ref, s32[4]{0:T(128)S(1)} %bitcast.53, bf16[640,1024]{1,0:T(8,128)(2,1)S(1)} %get-tuple-element.324.left_ref, bf16[1024,640]{1,0:T(8,128)(2,1)S(1)} %get-tuple-element.325.back_ref), custom_call_target="tpu_custom_call" | custom-call | flops 36800000000 | tf_op jit(solution)/shard_map/conv_gradient/pallas_call | solution.py:598
  92.3 7.6 %back_through_conv.1 = (bf16[1024,640]{1,0:T(8,128)(2,1)S(1)}, f32[1,640]{1,0:T(1,128)S(1)}, f32[1,640]{1,0:T(1,128)S(1)}, f32[1,640]{1,0:T(1,128)S(1)}) custom-call(bf16[1024,3200]{1,0:T(8,128)(2,1)S(1)} %get-tuple-element.329.taps_ref, bf16[640,3200]{1,0:T(8,128)(2,1)S(1)} %get-tuple-element.330.w_ref, f32[1024,640]{1,0:T(8,128)S(1)} %get-tuple-element.331.n_ref, ...), custom_call_target="tpu_custom_call" | custom-call | flops 46000001024 | tf_op jit(solution)/shard_map/back_through_conv/pallas_call | solution.py:621
  100.0 0.5 add_convert_fusion
  100.8 2.1 %collective-permute-start.22 = (bf16[4,208,128]{2,1,0:T(8,128)(2,1)S(1)}, bf16[4,208,128]{2,1,0:T(8,128)(2,1)S(1)}, u32[]{:S(2)}, u32[]{:S(2)}) collective-permute-start(bf16[4,208,128]{2,1,0:T(8,128)(2,1)S(1)} %get-tuple-element.346), channel_id=1, source_target_pairs={{0,16},{1,17},{2,18},{3,19},{4,20},{5,21},{6,22},{7,23},{8,9},{9,8... | collective-permute-start | bytes 638984 | tf_op jit(solution)/shard_map/ppermute | solution.py:820
  102.8 3.7 %in_gradient.1 = (bf16[16,208,128]{2,1,0:T(8,128)(2,1)S(1)}, bf16[16,208,128]{2,1,0:T(8,128)(2,1)S(1)}) custom-call(s32[2]{0:T(128)S(1)} %pad_add_fusion.me_ref, bf16[1280,1024]{1,0:T(8,128)(2,1)S(1)} %copy-done.20, bf16[1024,640]{1,0:T(8,128)(2,1)S(1)} %get-tuple-element.366.right_ref.back_ref), custom_call_target="tpu_custom_call" | custom-call | flops 17020000256 | tf_op jit(solution)/shard_map/in_gradient/pallas_call | solution.py:530
  106.7 3.8 %block_result.1 = bf16[1024,1280]{1,0:T(8,128)(2,1)} custom-call(bf16[1024,1280]{1,0:T(8,128)(2,1)S(1)} %bitcast.39, bf16[1024,640]{1,0:T(8,128)(2,1)S(1)} %copy-done.22, bf16[640,1280]{1,0:T(8,128)(2,1)S(1)} %get-tuple-element.353.w_ref, f32[1,7680]{1,0:T(1,128)S(1)} %reshape.100.vec_ref), custom_call_target="tpu_custom_call" | custom-call | flops 17479999488 | tf_op jit(solution)/shard_map/block_result/pallas_call | solution.py:575
  110.5 0.2 add_convert_fusion.4
  110.7 2.1 %collective-permute-start.20 = (bf16[8,208,128]{2,1,0:T(8,128)(2,1)S(1)}, bf16[8,208,128]{2,1,0:T(8,128)(2,1)S(1)}, u32[]{:S(2)}, u32[]{:S(2)}) collective-permute-start(bf16[8,208,128]{2,1,0:T(8,128)(2,1)S(1)} %get-tuple-element.361), channel_id=1, source_target_pairs={{0,2},{1,3},{2,0},{3,1},{4,6},{5,7},{6,4},{7,5},{8,12},{9,13},{10,... | collective-permute-start | bytes 1277960 | tf_op jit(solution)/shard_map/ppermute | solution.py:820
  112.8 2.6 %collective-permute-done.18 = bf16[8,512,128]{2,1,0:T(8,128)(2,1)S(1)} collective-permute-done((bf16[8,512,128]{2,1,0:T(8,128)(2,1)S(1)}, bf16[8,512,128]{2,1,0:T(8,128)(2,1)S(1)}, u32[]{:S(2)}, u32[]{:S(2)}) %collective-permute-start.18) | collective-permute-done | bytes 1048608 | tf_op jit(solution)/shard_map/ppermute | solution.py:820
  115.4 0.3 add_convert_fusion.2
  115.8 8.2 %back_through_in.1 = (bf16[1024,1280]{1,0:T(8,128)(2,1)}, f32[1,1280]{1,0:T(1,128)S(1)}, f32[1,1280]{1,0:T(1,128)S(1)}) custom-call(bf16[1024,640]{1,0:T(8,128)(2,1)S(1)} %get-tuple-element.366.right_ref.back_ref, bf16[1280,640]{1,0:T(8,128)(2,1)S(1)} %get-tuple-element.367.w_ref, bf16[1024,1280]{1,0:T(8,128)(2,1)S(1)} %bitcast.40, ...), custom_call_target="tpu_custom_call" | custom-call | flops 43240001536 | tf_op jit(solution)/shard_map/back_through_in/pallas_call | solution.py:655
  124.1 1.3 collective-permute-start.21
  125.4 0.1 add_convert_fusion.8
  125.6 1.6 collective-permute-start.26
  127.2 1.3 collective-permute-start.25
  128.6 2.2 %collective-permute-done.21 = bf16[4,208,128]{2,1,0:T(8,128)(2,1)S(1)} collective-permute-done((bf16[4,208,128]{2,1,0:T(8,128)(2,1)S(1)}, bf16[4,208,128]{2,1,0:T(8,128)(2,1)S(1)}, u32[]{:S(2)}, u32[]{:S(2)}) %collective-permute-start.21) | collective-permute-done | bytes 213024 | tf_op jit(solution)/shard_map/ppermute | solution.py:820
  130.8 2.9 %collective-permute-start.24 = (bf16[2,208,128]{2,1,0:T(8,128)(2,1)S(1)}, bf16[2,208,128]{2,1,0:T(8,128)(2,1)S(1)}, u32[]{:S(2)}, u32[]{:S(2)}) collective-permute-start(bf16[2,208,128]{2,1,0:T(8,128)(2,1)S(1)} %get-tuple-element.389), channel_id=1, source_target_pairs={{0,1},{1,0},{2,3},{3,2},{4,5},{5,4},{6,7},{7,6},{8,24},{9,25},{10,... | collective-permute-start | bytes 319496 | tf_op jit(solution)/shard_map/ppermute | solution.py:820
  133.8 1.8 %collective-permute-start.28 = (bf16[1,512,128]{2,1,0:T(8,128)(2,1)S(1)}, bf16[1,512,128]{2,1,0:T(8,128)(2,1)S(1)}, u32[]{:S(2)}, u32[]{:S(2)}) collective-permute-start(bf16[1,512,128]{2,1,0:T(8,128)(2,1)S(1)} %get-tuple-element.393), channel_id=1, source_target_pairs={{0,4},{1,5},{2,6},{3,7},{4,0},{5,1},{6,2},{7,3},{8,10},{9,11},{10,... | collective-permute-start | bytes 393224 | tf_op jit(solution)/shard_map/ppermute | solution.py:820
  135.6 1.3 collective-permute-start.29
  136.9 1.8 %collective-permute-start.27 = (bf16[1,208,128]{2,1,0:T(8,128)(2,1)S(1)}, bf16[1,208,128]{2,1,0:T(8,128)(2,1)S(1)}, u32[]{:S(2)}, u32[]{:S(2)}) collective-permute-start(bf16[1,208,128]{2,1,0:T(8,128)(2,1)S(1)} %get-tuple-element.401), channel_id=1, source_target_pairs={{0,4},{1,5},{2,6},{3,7},{4,0},{5,1},{6,2},{7,3},{8,10},{9,11},{10,... | collective-permute-start | bytes 159752 | tf_op jit(solution)/shard_map/ppermute | solution.py:820
  138.7 3.6 %collective-permute-done.29 = bf16[1,208,128]{2,1,0:T(8,128)(2,1)S(1)} collective-permute-done((bf16[1,208,128]{2,1,0:T(8,128)(2,1)S(1)}, bf16[1,208,128]{2,1,0:T(8,128)(2,1)S(1)}, u32[]{:S(2)}, u32[]{:S(2)}) %collective-permute-start.29) | collective-permute-done | bytes 53280 | tf_op jit(solution)/shard_map/ppermute | solution.py:820
  142.3 1.1 collective-permute-done.27
  143.8 1.2 collective-permute-done.30
  145.0 0.4 collective-permute-start.31
  145.4 4.4 %collective-permute-done.31 = f32[64,128]{1,0:T(8,128)S(1)} collective-permute-done((f32[64,128]{1,0:T(8,128)S(1)}, f32[64,128]{1,0:T(8,128)S(1)}, u32[]{:S(2)}, u32[]{:S(2)}) %collective-permute-start.31) | collective-permute-done | bytes 32800 | tf_op jit(solution)/shard_map/ppermute | solution.py:834
  150.0 3.8 %collective-permute-done.32 = f32[64,128]{1,0:T(8,128)S(1)} collective-permute-done((f32[64,128]{1,0:T(8,128)S(1)}, f32[64,128]{1,0:T(8,128)S(1)}, u32[]{:S(2)}, u32[]{:S(2)}) %collective-permute-start.32) | collective-permute-done | bytes 32800 | tf_op jit(solution)/shard_map/ppermute | solution.py:834
  153.7 1.2 collective-permute-start.33
  154.9 2.8 %collective-permute-done.33 = f32[64,128]{1,0:T(8,128)S(1)} collective-permute-done((f32[64,128]{1,0:T(8,128)S(1)}, f32[64,128]{1,0:T(8,128)S(1)}, u32[]{:S(2)}, u32[]{:S(2)}) %collective-permute-start.33) | collective-permute-done | bytes 32800 | tf_op jit(solution)/shard_map/ppermute | solution.py:834
  157.7 1.2 collective-permute-start.34
  158.9 2.7 %collective-permute-done.34 = f32[64,128]{1,0:T(8,128)S(1)} collective-permute-done((f32[64,128]{1,0:T(8,128)S(1)}, f32[64,128]{1,0:T(8,128)S(1)}, u32[]{:S(2)}, u32[]{:S(2)}) %collective-permute-start.34) | collective-permute-done | bytes 32800 | tf_op jit(solution)/shard_map/ppermute | solution.py:834
  161.8 2.1 %update_all.1 = (f32[1,1]{1,0:T(1,128)}, f32[160,160]{1,0:T(8,128)}, f32[160,160]{1,0:T(8,128)}, f32[160,160]{1,0:T(8,128)}, f32[400,160]{1,0:T(8,128)}, /*index...) custom-call(f32[208,128]{1,0:T(8,128)S(1)} %get-tuple-element.451.re, ...), custom_call_target="tpu_custom_call" | custom-call | flops 9200000000 | tf_op jit(solution)/shard_map/update_all/pallas_call | solution.py:746
  (121 shorter events, 2.8 us)
Async XLA Ops:
  0.6 5.1 %copy-start.5 = (f32[5,80,160]{2,1,0:T(8,128)S(1)}, f32[5,80,160]{2,1,0:T(8,128)}, u32[]{:S(2)}) copy-start(f32[5,80,160]{2,1,0:T(8,128)} %param.21) | copy-start | bytes 768004
  0.7 1.0 copy-start.9
  1.7 11.3 %collective-permute-start.1 = (bf16[1,208,128]{2,1,0:T(8,128)(2,1)S(1)}, bf16[1,208,128]{2,1,0:T(8,128)(2,1)}, u32[]{:S(2)}, u32[]{:S(2)}) collective-permute-start(bf16[1,208,128]{2,1,0:T(8,128)(2,1)S(1)} %bitcast.34), channel_id=1, source_target_pairs={{0,4},{1,5},{2,6},{3,7},{4,0},{5,1},{6,2},{7,3},{8,10},{9,11},{10,... | collective-permute-start | bytes 159752 | tf_op jit(solution)/shard_map/ppermute | solution.py:782
  5.8 0.8 copy-start
  5.8 0.9 copy-start.13
  5.9 9.5 %collective-permute-start = (bf16[1,512,128]{2,1,0:T(8,128)(2,1)S(1)}, bf16[1,512,128]{2,1,0:T(8,128)(2,1)S(1)}, u32[]{:S(2)}, u32[]{:S(2)}) collective-permute-start(bf16[1,512,128]{2,1,0:T(8,128)(2,1)S(1)} %bitcast.30), channel_id=1, source_target_pairs={{0,4},{1,5},{2,6},{3,7},{4,0},{5,1},{6,2},{7,3},{8,10},{9,11},{10,... | collective-permute-start | bytes 393224 | tf_op jit(solution)/shard_map/ppermute | solution.py:782
  6.7 0.7 copy-start.25
  6.7 1.8 %copy-start.2 = (bf16[1,1024,1280]{2,1,0:T(8,128)(2,1)S(1)}, bf16[1,1024,1280]{2,1,0:T(8,128)(2,1)}, u32[]{:S(2)}) copy-start(bf16[1,1024,1280]{2,1,0:T(8,128)(2,1)} %param.15) | copy-start | bytes 7864324
  8.5 1.7 %copy-start.3 = (bf16[1,1024,1280]{2,1,0:T(8,128)(2,1)S(1)}, bf16[1,1024,1280]{2,1,0:T(8,128)(2,1)}, u32[]{:S(2)}) copy-start(bf16[1,1024,1280]{2,1,0:T(8,128)(2,1)} %param.16) | copy-start | bytes 7864324
  13.9 8.3 %collective-permute-start.3 = (bf16[2,208,128]{2,1,0:T(8,128)(2,1)S(1)}, bf16[2,208,128]{2,1,0:T(8,128)(2,1)S(1)}, u32[]{:S(2)}, u32[]{:S(2)}) collective-permute-start(bf16[2,208,128]{2,1,0:T(8,128)(2,1)S(1)} %constant_dynamic-update-slice_fusion), channel_id=1, source_target_pairs={{0,1},{1,0},{2,3},{3,2},{4,5},{5,4},{6,7},{7,6},{8,24},{9,25},{10,... | collective-permute-start | bytes 319496 | tf_op jit(solution)/shard_map/ppermute | solution.py:782
  15.5 11.0 %collective-permute-start.6 = (bf16[1,208,128]{2,1,0:T(8,128)(2,1)S(1)}, bf16[1,208,128]{2,1,0:T(8,128)(2,1)S(1)}, u32[]{:S(2)}, u32[]{:S(2)}) collective-permute-start(bf16[1,208,128]{2,1,0:T(8,128)(2,1)S(1)} %bitcast.32), channel_id=1, source_target_pairs={{0,4},{1,5},{2,6},{3,7},{4,0},{5,1},{6,2},{7,3},{8,10},{9,11},{10,... | collective-permute-start | bytes 159752 | tf_op jit(solution)/shard_map/ppermute | solution.py:782
  17.7 8.7 %collective-permute-start.2 = (bf16[2,512,128]{2,1,0:T(8,128)(2,1)S(1)}, bf16[2,512,128]{2,1,0:T(8,128)(2,1)S(1)}, u32[]{:S(2)}, u32[]{:S(2)}) collective-permute-start(bf16[2,512,128]{2,1,0:T(8,128)(2,1)S(1)} %constant_dynamic-update-slice_fusion.2), channel_id=1, source_target_pairs={{0,2},{1,3},{2,0},{3,1},{4,6},{5,7},{6,4},{7,5},{8,12},{9,13},{10,... | collective-permute-start | bytes 786440 | tf_op jit(solution)/shard_map/ppermute | solution.py:782
  22.1 13.7 %copy-start.19 = (bf16[1280,1024]{1,0:T(8,128)(2,1)}, bf16[1280,1024]{1,0:T(8,128)(2,1)S(1)}, u32[]{:S(2)}) copy-start(bf16[1280,1024]{1,0:T(8,128)(2,1)S(1)} %get-tuple-element.348.left_ref) | copy-start | bytes 7864324
  22.1 13.7 %copy-start.23 = (f32[1024,128]{1,0:T(8,128)}, f32[1024,128]{1,0:T(8,128)S(1)}, u32[]{:S(2)}) copy-start(f32[1024,128]{1,0:T(8,128)S(1)} %get-tuple-element.370.stat_ref) | copy-start | bytes 1572868
  22.2 6.7 %collective-permute-start.5 = (bf16[4,208,128]{2,1,0:T(8,128)(2,1)S(1)}, bf16[4,208,128]{2,1,0:T(8,128)(2,1)S(1)}, u32[]{:S(2)}, u32[]{:S(2)}) collective-permute-start(bf16[4,208,128]{2,1,0:T(8,128)(2,1)S(1)} %constant_dynamic-update-slice_fusion.4), channel_id=1, source_target_pairs={{0,16},{1,17},{2,18},{3,19},{4,20},{5,21},{6,22},{7,23},{8,9},{9,8... | collective-permute-start | bytes 638984 | tf_op jit(solution)/shard_map/ppermute | solution.py:782
  26.5 9.2 %collective-permute-start.4 = (bf16[4,512,128]{2,1,0:T(8,128)(2,1)S(1)}, bf16[4,512,128]{2,1,0:T(8,128)(2,1)S(1)}, u32[]{:S(2)}, u32[]{:S(2)}) collective-permute-start(bf16[4,512,128]{2,1,0:T(8,128)(2,1)S(1)} %constant_dynamic-update-slice_fusion.6), channel_id=1, source_target_pairs={{0,1},{1,0},{2,3},{3,2},{4,5},{5,4},{6,7},{7,6},{8,24},{9,25},{10,... | collective-permute-start | bytes 1572872 | tf_op jit(solution)/shard_map/ppermute | solution.py:782
  28.9 12.3 %collective-permute-start.9 = (bf16[8,208,128]{2,1,0:T(8,128)(2,1)S(1)}, bf16[8,208,128]{2,1,0:T(8,128)(2,1)S(1)}, u32[]{:S(2)}, u32[]{:S(2)}) collective-permute-start(bf16[8,208,128]{2,1,0:T(8,128)(2,1)S(1)} %constant_dynamic-update-slice_fusion.10), channel_id=1, source_target_pairs={{0,2},{1,3},{2,0},{3,1},{4,6},{5,7},{6,4},{7,5},{8,12},{9,13},{10,... | collective-permute-start | bytes 1277960 | tf_op jit(solution)/shard_map/ppermute | solution.py:782
  41.3 2.6 %collective-permute-start.10 = (bf16[16,208,128]{2,1,0:T(8,128)(2,1)S(1)}, bf16[16,208,128]{2,1,0:T(8,128)(2,1)S(1)}, u32[]{:S(2)}, u32[]{:S(2)}) collective-permute-start(bf16[16,208,128]{2,1,0:T(8,128)(2,1)S(1)} %constant_dynamic-update-slice_fusion.14.own_ref), channel_id=1, source_target_pairs={{0,8},{1,9},{2,10},{3,11},{4,12},{5,13},{6,14},{7,15},{8,0},{9,1},... | collective-permute-start | bytes 2555912 | tf_op jit(solution)/shard_map/ppermute | solution.py:782
  41.4 15.3 %collective-permute-start.7 = (bf16[8,512,128]{2,1,0:T(8,128)(2,1)S(1)}, bf16[8,512,128]{2,1,0:T(8,128)(2,1)S(1)}, u32[]{:S(2)}, u32[]{:S(2)}) collective-permute-start(bf16[8,512,128]{2,1,0:T(8,128)(2,1)S(1)} %constant_dynamic-update-slice_fusion.12), channel_id=1, source_target_pairs={{0,16},{1,17},{2,18},{3,19},{4,20},{5,21},{6,22},{7,23},{8,9},{9,8... | collective-permute-start | bytes 3145736 | tf_op jit(solution)/shard_map/ppermute | solution.py:782
  43.9 8.6 %collective-permute-start.8 = (bf16[2,208,128]{2,1,0:T(8,128)(2,1)S(1)}, bf16[2,208,128]{2,1,0:T(8,128)(2,1)S(1)}, u32[]{:S(2)}, u32[]{:S(2)}) collective-permute-start(bf16[2,208,128]{2,1,0:T(8,128)(2,1)S(1)} %constant_dynamic-update-slice_fusion.8), channel_id=1, source_target_pairs={{0,2},{1,3},{2,0},{3,1},{4,6},{5,7},{6,4},{7,5},{8,12},{9,13},{10,... | collective-permute-start | bytes 319496 | tf_op jit(solution)/shard_map/ppermute | solution.py:782
  56.9 4.2 %collective-permute-start.11 = (bf16[16,512,128]{2,1,0:T(8,128)(2,1)S(1)}, bf16[16,512,128]{2,1,0:T(8,128)(2,1)S(1)}, u32[]{:S(2)}, u32[]{:S(2)}) collective-permute-start(bf16[16,512,128]{2,1,0:T(8,128)(2,1)S(1)} %constant_dynamic-update-slice_fusion.18.own_ref), channel_id=1, source_target_pairs={{0,8},{1,9},{2,10},{3,11},{4,12},{5,13},{6,14},{7,15},{8,0},{9,1},... | collective-permute-start | bytes 6291464 | tf_op jit(solution)/shard_map/ppermute | solution.py:782
  57.0 5.9 %collective-permute-start.12 = (bf16[4,208,128]{2,1,0:T(8,128)(2,1)S(1)}, bf16[4,208,128]{2,1,0:T(8,128)(2,1)S(1)}, u32[]{:S(2)}, u32[]{:S(2)}) collective-permute-start(bf16[4,208,128]{2,1,0:T(8,128)(2,1)S(1)} %constant_dynamic-update-slice_fusion.16), channel_id=1, source_target_pairs={{0,1},{1,0},{2,3},{3,2},{4,5},{5,4},{6,7},{7,6},{8,24},{9,25},{10,... | collective-permute-start | bytes 638984 | tf_op jit(solution)/shard_map/ppermute | solution.py:782
  63.0 11.1 %copy-start.4 = (bf16[1,1024,1280]{2,1,0:T(8,128)(2,1)S(1)}, bf16[1,1024,1280]{2,1,0:T(8,128)(2,1)}, u32[]{:S(2)}) copy-start(bf16[1,1024,1280]{2,1,0:T(8,128)(2,1)} %param.16) | copy-start | bytes 7864324
  63.0 10.9 %collective-permute-start.13 = (bf16[8,208,128]{2,1,0:T(8,128)(2,1)S(1)}, bf16[8,208,128]{2,1,0:T(8,128)(2,1)S(1)}, u32[]{:S(2)}, u32[]{:S(2)}) collective-permute-start(bf16[8,208,128]{2,1,0:T(8,128)(2,1)S(1)} %constant_dynamic-update-slice_fusion.20), channel_id=1, source_target_pairs={{0,16},{1,17},{2,18},{3,19},{4,20},{5,21},{6,22},{7,23},{8,9},{9,8... | collective-permute-start | bytes 1277960 | tf_op jit(solution)/shard_map/ppermute | solution.py:782
  73.8 3.2 %copy-start.21 = (bf16[1024,640]{1,0:T(8,128)(2,1)}, bf16[1024,640]{1,0:T(8,128)(2,1)S(1)}, u32[]{:S(2)}) copy-start(bf16[1024,640]{1,0:T(8,128)(2,1)S(1)} %get-tuple-element.352.h_ref) | copy-start | bytes 3932164
  74.0 3.7 %collective-permute-start.14 = (bf16[16,208,128]{2,1,0:T(8,128)(2,1)S(1)}, bf16[16,208,128]{2,1,0:T(8,128)(2,1)S(1)}, u32[]{:S(2)}, u32[]{:S(2)}) collective-permute-start(bf16[16,208,128]{2,1,0:T(8,128)(2,1)S(1)} %constant_dynamic-update-slice_fusion.22.own_ref), channel_id=1, source_target_pairs={{0,8},{1,9},{2,10},{3,11},{4,12},{5,13},{6,14},{7,15},{8,0},{9,1},... | collective-permute-start | bytes 2555912 | tf_op jit(solution)/shard_map/ppermute | solution.py:782
  77.1 6.6 %collective-permute-start.15 = (bf16[16,208,128]{2,1,0:T(8,128)(2,1)S(1)}, bf16[16,208,128]{2,1,0:T(8,128)(2,1)S(1)}, u32[]{:S(2)}, u32[]{:S(2)}) collective-permute-start(bf16[16,208,128]{2,1,0:T(8,128)(2,1)S(1)} %get-tuple-element.317), channel_id=1, source_target_pairs={{0,8},{1,9},{2,10},{3,11},{4,12},{5,13},{6,14},{7,15},{8,0},{9,1},... | collective-permute-start | bytes 2555912 | tf_op jit(solution)/shard_map/ppermute | solution.py:810
  83.9 16.7 %collective-permute-start.16 = (bf16[8,208,128]{2,1,0:T(8,128)(2,1)S(1)}, bf16[8,208,128]{2,1,0:T(8,128)(2,1)S(1)}, u32[]{:S(2)}, u32[]{:S(2)}) collective-permute-start(bf16[8,208,128]{2,1,0:T(8,128)(2,1)S(1)} %get-tuple-element.321), channel_id=1, source_target_pairs={{0,2},{1,3},{2,0},{3,1},{4,6},{5,7},{6,4},{7,5},{8,12},{9,13},{10,... | collective-permute-start | bytes 1277960 | tf_op jit(solution)/shard_map/ppermute | solution.py:820
  92.2 7.7 %collective-permute-start.17 = (bf16[16,512,128]{2,1,0:T(8,128)(2,1)S(1)}, bf16[16,512,128]{2,1,0:T(8,128)(2,1)S(1)}, u32[]{:S(2)}, u32[]{:S(2)}) collective-permute-start(bf16[16,512,128]{2,1,0:T(8,128)(2,1)S(1)} %get-tuple-element.337), channel_id=1, source_target_pairs={{0,8},{1,9},{2,10},{3,11},{4,12},{5,13},{6,14},{7,15},{8,0},{9,1},... | collective-permute-start | bytes 6291464 | tf_op jit(solution)/shard_map/ppermute | solution.py:810
  100.0 2.9 %copy-start.20 = (bf16[1280,1024]{1,0:T(8,128)(2,1)S(1)}, bf16[1280,1024]{1,0:T(8,128)(2,1)}, u32[]{:S(2)}) copy-start(bf16[1280,1024]{1,0:T(8,128)(2,1)} %copy-done.19) | copy-start | bytes 7864324
  100.5 14.9 %collective-permute-start.18 = (bf16[8,512,128]{2,1,0:T(8,128)(2,1)S(1)}, bf16[8,512,128]{2,1,0:T(8,128)(2,1)S(1)}, u32[]{:S(2)}, u32[]{:S(2)}) collective-permute-start(bf16[8,512,128]{2,1,0:T(8,128)(2,1)S(1)} %get-tuple-element.342), channel_id=1, source_target_pairs={{0,16},{1,17},{2,18},{3,19},{4,20},{5,21},{6,22},{7,23},{8,9},{9,8... | collective-permute-start | bytes 3145736 | tf_op jit(solution)/shard_map/ppermute | solution.py:820
  100.8 26.4 %collective-permute-start.22 = (bf16[4,208,128]{2,1,0:T(8,128)(2,1)S(1)}, bf16[4,208,128]{2,1,0:T(8,128)(2,1)S(1)}, u32[]{:S(2)}, u32[]{:S(2)}) collective-permute-start(bf16[4,208,128]{2,1,0:T(8,128)(2,1)S(1)} %get-tuple-element.346), channel_id=1, source_target_pairs={{0,16},{1,17},{2,18},{3,19},{4,20},{5,21},{6,22},{7,23},{8,9},{9,8... | collective-permute-start | bytes 638984 | tf_op jit(solution)/shard_map/ppermute | solution.py:820
  102.8 3.8 %copy-start.22 = (bf16[1024,640]{1,0:T(8,128)(2,1)S(1)}, bf16[1024,640]{1,0:T(8,128)(2,1)}, u32[]{:S(2)}) copy-start(bf16[1024,640]{1,0:T(8,128)(2,1)} %copy-done.21) | copy-start | bytes 3932164
  106.6 3.9 %collective-permute-start.19 = (bf16[16,208,128]{2,1,0:T(8,128)(2,1)S(1)}, bf16[16,208,128]{2,1,0:T(8,128)(2,1)S(1)}, u32[]{:S(2)}, u32[]{:S(2)}) collective-permute-start(bf16[16,208,128]{2,1,0:T(8,128)(2,1)S(1)} %get-tuple-element.357), channel_id=1, source_target_pairs={{0,8},{1,9},{2,10},{3,11},{4,12},{5,13},{6,14},{7,15},{8,0},{9,1},... | collective-permute-start | bytes 2555912 | tf_op jit(solution)/shard_map/ppermute | solution.py:810
  110.7 5.1 %copy-start.24 = (f32[1024,128]{1,0:T(8,128)S(1)}, f32[1024,128]{1,0:T(8,128)}, u32[]{:S(2)}) copy-start(f32[1024,128]{1,0:T(8,128)} %copy-done.23) | copy-start | bytes 1572868
  110.7 13.3 %collective-permute-start.20 = (bf16[8,208,128]{2,1,0:T(8,128)(2,1)S(1)}, bf16[8,208,128]{2,1,0:T(8,128)(2,1)S(1)}, u32[]{:S(2)}, u32[]{:S(2)}) collective-permute-start(bf16[8,208,128]{2,1,0:T(8,128)(2,1)S(1)} %get-tuple-element.361), channel_id=1, source_target_pairs={{0,2},{1,3},{2,0},{3,1},{4,6},{5,7},{6,4},{7,5},{8,12},{9,13},{10,... | collective-permute-start | bytes 1277960 | tf_op jit(solution)/shard_map/ppermute | solution.py:820
  115.7 9.7 %collective-permute-start.23 = (bf16[4,512,128]{2,1,0:T(8,128)(2,1)S(1)}, bf16[4,512,128]{2,1,0:T(8,128)(2,1)S(1)}, u32[]{:S(2)}, u32[]{:S(2)}) collective-permute-start(bf16[4,512,128]{2,1,0:T(8,128)(2,1)S(1)} %get-tuple-element.365), channel_id=1, source_target_pairs={{0,1},{1,0},{2,3},{3,2},{4,5},{5,4},{6,7},{7,6},{8,24},{9,25},{10,... | collective-permute-start | bytes 1572872 | tf_op jit(solution)/shard_map/ppermute | solution.py:820
  124.1 6.6 %collective-permute-start.21 = (bf16[4,208,128]{2,1,0:T(8,128)(2,1)S(1)}, bf16[4,208,128]{2,1,0:T(8,128)(2,1)S(1)}, u32[]{:S(2)}, u32[]{:S(2)}) collective-permute-start(bf16[4,208,128]{2,1,0:T(8,128)(2,1)S(1)} %get-tuple-element.377), channel_id=1, source_target_pairs={{0,16},{1,17},{2,18},{3,19},{4,20},{5,21},{6,22},{7,23},{8,9},{9,8... | collective-permute-start | bytes 638984 | tf_op jit(solution)/shard_map/ppermute | solution.py:820
  125.6 8.1 %collective-permute-start.26 = (bf16[2,512,128]{2,1,0:T(8,128)(2,1)S(1)}, bf16[2,512,128]{2,1,0:T(8,128)(2,1)S(1)}, u32[]{:S(2)}, u32[]{:S(2)}) collective-permute-start(bf16[2,512,128]{2,1,0:T(8,128)(2,1)S(1)} %get-tuple-element.381), channel_id=1, source_target_pairs={{0,2},{1,3},{2,0},{3,1},{4,6},{5,7},{6,4},{7,5},{8,12},{9,13},{10,... | collective-permute-start | bytes 786440 | tf_op jit(solution)/shard_map/ppermute | solution.py:820
  127.2 8.3 %collective-permute-start.25 = (bf16[2,208,128]{2,1,0:T(8,128)(2,1)S(1)}, bf16[2,208,128]{2,1,0:T(8,128)(2,1)S(1)}, u32[]{:S(2)}, u32[]{:S(2)}) collective-permute-start(bf16[2,208,128]{2,1,0:T(8,128)(2,1)S(1)} %get-tuple-element.385), channel_id=1, source_target_pairs={{0,1},{1,0},{2,3},{3,2},{4,5},{5,4},{6,7},{7,6},{8,24},{9,25},{10,... | collective-permute-start | bytes 319496 | tf_op jit(solution)/shard_map/ppermute | solution.py:820
  130.8 6.1 %collective-permute-start.24 = (bf16[2,208,128]{2,1,0:T(8,128)(2,1)S(1)}, bf16[2,208,128]{2,1,0:T(8,128)(2,1)S(1)}, u32[]{:S(2)}, u32[]{:S(2)}) collective-permute-start(bf16[2,208,128]{2,1,0:T(8,128)(2,1)S(1)} %get-tuple-element.389), channel_id=1, source_target_pairs={{0,1},{1,0},{2,3},{3,2},{4,5},{5,4},{6,7},{7,6},{8,24},{9,25},{10,... | collective-permute-start | bytes 319496 | tf_op jit(solution)/shard_map/ppermute | solution.py:820
  133.8 9.7 %collective-permute-start.28 = (bf16[1,512,128]{2,1,0:T(8,128)(2,1)S(1)}, bf16[1,512,128]{2,1,0:T(8,128)(2,1)S(1)}, u32[]{:S(2)}, u32[]{:S(2)}) collective-permute-start(bf16[1,512,128]{2,1,0:T(8,128)(2,1)S(1)} %get-tuple-element.393), channel_id=1, source_target_pairs={{0,4},{1,5},{2,6},{3,7},{4,0},{5,1},{6,2},{7,3},{8,10},{9,11},{10,... | collective-permute-start | bytes 393224 | tf_op jit(solution)/shard_map/ppermute | solution.py:820
  135.6 6.7 %collective-permute-start.29 = (bf16[1,208,128]{2,1,0:T(8,128)(2,1)S(1)}, bf16[1,208,128]{2,1,0:T(8,128)(2,1)S(1)}, u32[]{:S(2)}, u32[]{:S(2)}) collective-permute-start(bf16[1,208,128]{2,1,0:T(8,128)(2,1)S(1)} %get-tuple-element.397), channel_id=1, source_target_pairs={{0,4},{1,5},{2,6},{3,7},{4,0},{5,1},{6,2},{7,3},{8,10},{9,11},{10,... | collective-permute-start | bytes 159752 | tf_op jit(solution)/shard_map/ppermute | solution.py:820
  136.9 6.5 %collective-permute-start.27 = (bf16[1,208,128]{2,1,0:T(8,128)(2,1)S(1)}, bf16[1,208,128]{2,1,0:T(8,128)(2,1)S(1)}, u32[]{:S(2)}, u32[]{:S(2)}) collective-permute-start(bf16[1,208,128]{2,1,0:T(8,128)(2,1)S(1)} %get-tuple-element.401), channel_id=1, source_target_pairs={{0,4},{1,5},{2,6},{3,7},{4,0},{5,1},{6,2},{7,3},{8,10},{9,11},{10,... | collective-permute-start | bytes 159752 | tf_op jit(solution)/shard_map/ppermute | solution.py:820
  143.5 18.2 %copy-start.1 = (f32[7680]{0:T(1024)S(1)}, f32[7680]{0:T(1024)}, u32[]{:S(2)}) copy-start(f32[7680]{0:T(1024)} %param.27) | copy-start | bytes 92164
  143.5 18.2 %copy-start.6 = (f32[5,80,160]{2,1,0:T(8,128)S(1)}, f32[5,80,160]{2,1,0:T(8,128)}, u32[]{:S(2)}) copy-start(f32[5,80,160]{2,1,0:T(8,128)} %param.21) | copy-start | bytes 768004
  143.5 18.2 %copy-start.7 = (f32[5,80,160]{2,1,0:T(8,128)S(1)}, f32[5,80,160]{2,1,0:T(8,128)}, u32[]{:S(2)}) copy-start(f32[5,80,160]{2,1,0:T(8,128)} %param.22) | copy-start | bytes 768004
  143.5 18.2 %copy-start.8 = (f32[5,80,160]{2,1,0:T(8,128)S(1)}, f32[5,80,160]{2,1,0:T(8,128)}, u32[]{:S(2)}) copy-start(f32[5,80,160]{2,1,0:T(8,128)} %param.23) | copy-start | bytes 768004
  143.5 18.2 %copy-start.10 = (f32[160,160]{1,0:T(8,128)S(1)}, f32[160,160]{1,0:T(8,128)}, u32[]{:S(2)}) copy-start(f32[160,160]{1,0:T(8,128)} %refs_4_.1) | copy-start | bytes 307204
  143.5 18.2 %copy-start.11 = (f32[160,160]{1,0:T(8,128)S(1)}, f32[160,160]{1,0:T(8,128)}, u32[]{:S(2)}) copy-start(f32[160,160]{1,0:T(8,128)} %refs_5_.1) | copy-start | bytes 307204
  143.6 18.2 %copy-start.12 = (f32[160,160]{1,0:T(8,128)S(1)}, f32[160,160]{1,0:T(8,128)}, u32[]{:S(2)}) copy-start(f32[160,160]{1,0:T(8,128)} %refs_6_.1) | copy-start | bytes 307204
  143.6 18.2 %copy-start.14 = (f32[80,320]{1,0:T(8,128)S(1)}, f32[80,320]{1,0:T(8,128)}, u32[]{:S(2)}) copy-start(f32[80,320]{1,0:T(8,128)} %refs_10_.1) | copy-start | bytes 307204
  143.6 18.2 %copy-start.15 = (f32[80,320]{1,0:T(8,128)S(1)}, f32[80,320]{1,0:T(8,128)}, u32[]{:S(2)}) copy-start(f32[80,320]{1,0:T(8,128)} %refs_11_.1) | copy-start | bytes 307204
  143.6 18.2 %copy-start.16 = (f32[80,320]{1,0:T(8,128)S(1)}, f32[80,320]{1,0:T(8,128)}, u32[]{:S(2)}) copy-start(f32[80,320]{1,0:T(8,128)} %refs_12_.1) | copy-start | bytes 307204
  143.6 18.2 %copy-start.17 = (f32[7680]{0:T(1024)S(1)}, f32[7680]{0:T(1024)}, u32[]{:S(2)}) copy-start(f32[7680]{0:T(1024)} %param.28) | copy-start | bytes 92164
  143.6 18.2 %copy-start.18 = (f32[7680]{0:T(1024)S(1)}, f32[7680]{0:T(1024)}, u32[]{:S(2)}) copy-start(f32[7680]{0:T(1024)} %param.29) | copy-start | bytes 92164
  143.7 1.3 collective-permute-start.30
  145.0 4.8 %collective-permute-start.31 = (f32[64,128]{1,0:T(8,128)S(1)}, f32[64,128]{1,0:T(8,128)S(1)}, u32[]{:S(2)}, u32[]{:S(2)}) collective-permute-start(f32[64,128]{1,0:T(8,128)S(1)} %add.127), channel_id=1, source_target_pairs={{0,4},{1,5},{2,6},{3,7},{4,0},{5,1},{6,2},{7,3},{8,10},{9,11},{10,... | collective-permute-start | bytes 98312 | tf_op jit(solution)/shard_map/ppermute | solution.py:834
  149.8 3.9 %collective-permute-start.32 = (f32[64,128]{1,0:T(8,128)S(1)}, f32[64,128]{1,0:T(8,128)S(1)}, u32[]{:S(2)}, u32[]{:S(2)}) collective-permute-start(f32[64,128]{1,0:T(8,128)S(1)} %add.128), channel_id=1, source_target_pairs={{0,2},{1,3},{2,0},{3,1},{4,6},{5,7},{6,4},{7,5},{8,12},{9,13},{10,... | collective-permute-start | bytes 98312 | tf_op jit(solution)/shard_map/ppermute | solution.py:834
  153.7 4.0 %collective-permute-start.33 = (f32[64,128]{1,0:T(8,128)S(1)}, f32[64,128]{1,0:T(8,128)S(1)}, u32[]{:S(2)}, u32[]{:S(2)}) collective-permute-start(f32[64,128]{1,0:T(8,128)S(1)} %add.129), channel_id=1, source_target_pairs={{0,1},{1,0},{2,3},{3,2},{4,5},{5,4},{6,7},{7,6},{8,24},{9,25},{10,... | collective-permute-start | bytes 98312 | tf_op jit(solution)/shard_map/ppermute | solution.py:834
  157.7 3.9 %collective-permute-start.34 = (f32[64,128]{1,0:T(8,128)S(1)}, f32[64,128]{1,0:T(8,128)S(1)}, u32[]{:S(2)}, u32[]{:S(2)}) collective-permute-start(f32[64,128]{1,0:T(8,128)S(1)} %add.130), channel_id=1, source_target_pairs={{0,16},{1,17},{2,18},{3,19},{4,20},{5,21},{6,22},{7,23},{8,9},{9,8... | collective-permute-start | bytes 98312 | tf_op jit(solution)/shard_map/ppermute | solution.py:834
